TPU v7x, 32 devices: a whole 2x2x4 slice. The times are simulated.
32 devices in a mesh: groups: 2 (over y), block: 8 (over z, core), dp: 1, seq: 2 (over x).
Axes of the slice: x: 2, y: 2, z: 4, core: 2. Of those that a mesh axis runs over, the one named last changes fastest.
Arguments:
- inputs: float32 [4096, 2, 1024], P('block', 'groups', ('dp', 'seq')), parts along dimension 1, may hold values from -6 to 6
- cotangent: float32 [4096, 2, 1024], P('block', 'groups', ('dp', 'seq')), parts along dimension 1, may hold values from -6 to 6
- seq_right: float32 [8, 128, 128], P(('dp', 'seq')), may hold values from -0.5 to 0.5
- seq_left: float32 [128, 8, 8], P(('dp', 'seq')), may hold values from -2 to 2
- seq_gain: float32 [4096], P('block'), may hold values from 0.5 to 2
- gate_right: float32 [64, 64, 64], P('block'), may hold values from -0.75 to 0.75
- gate_left: float32 [64, 64, 64], P('block'), may hold values from -0.75 to 0.75
- value_right: float32 [64, 64, 64], P('block'), may hold values from -0.75 to 0.75
- value_left: float32 [64, 64, 64], P('block'), may hold values from -0.75 to 0.75
- output_right: float32 [64, 64, 64], P('block'), may hold values from -0.75 to 0.75
- output_left: float32 [64, 64, 64], P('block'), may hold values from -0.75 to 0.75
Outputs:
- layer_out: float32 [4096, 2, 1024], P('block', 'groups', ('dp', 'seq')), parts along dimension 1
- grad_inputs: float32 [4096, 2, 1024], P('block', 'groups', ('dp', 'seq')), parts along dimension 1
- grad_seq_right: float32 [16, 128, 128], P(('groups', 'dp', 'seq')), parts along dimension 0
- grad_seq_left: float32 [256, 8, 8], P(('groups', 'dp', 'seq')), parts along dimension 0
- grad_seq_gain: float32 [8192], P(('groups', 'block')), parts along dimension 0
- grad_gate_right: float32 [128, 64, 64], P(('groups', 'block')), parts along dimension 0
- grad_gate_left: float32 [128, 64, 64], P(('groups', 'block')), parts along dimension 0
- grad_value_right: float32 [128, 64, 64], P(('groups', 'block')), parts along dimension 0
- grad_value_left: float32 [128, 64, 64], P(('groups', 'block')), parts along dimension 0
- grad_output_right: float32 [128, 64, 64], P(('groups', 'block')), parts along dimension 0
- grad_output_left: float32 [128, 64, 64], P(('groups', 'block')), parts along dimension 0
There are 2 independent parts, one for each index of `groups`. A program takes and returns all parts, laid end to end along the dimension named above; an argument that names none is the same for every part. Nothing has to cross between parts.
All inputs are finite; a program needn't handle non-finite values.
Results may differ from a plain program's by a relative error of at most 0.00017.
Values sent between devices are 32-bit elements; how exact they have to be, the bound alone decides.
A program may use at most 64 MiB of HBM per device.

v0:
```python
import math

import jax
import jax.numpy as jnp
from jax import lax
from jax.sharding import PartitionSpec as P

precise = lax.Precision.HIGHEST


def contract(pattern, former, latter):
    return jnp.einsum(pattern, former, latter, precision=precise)


def gated(gate_in, value_in):
    return jax.nn.gelu(gate_in) * value_in


def body(
    inputs,
    cotangent,
    seq_right,
    seq_left,
    seq_gain,
    gate_right,
    gate_left,
    value_right,
    value_left,
    output_right,
    output_left,
):
    channels = inputs.shape[0]
    length = inputs.shape[1] * inputs.shape[2]
    source = inputs.reshape(channels, length)
    upstream = cotangent.reshape(channels, length)
    blocks_here = gate_right.shape[0]
    breadth = gate_right.shape[1]
    seq_here = seq_right.shape[0]
    seq_block = seq_right.shape[1]
    seq_source = source.reshape(channels, seq_here, seq_block)
    sectioned_seq = contract("cai,aij->caj", seq_source, seq_right)
    portion = lax.all_to_all(sectioned_seq, ("dp", "seq"), split_axis=2, concat_axis=1, tiled=True)
    mixed_across = contract("caj,jab->cbj", portion, seq_left)
    seq_mixed = lax.all_to_all(
        mixed_across, ("dp", "seq"), split_axis=1, concat_axis=2, tiled=True
    ).reshape(channels, length)
    mixed_in = source + seq_gain[:, None] * seq_mixed

    def apply_right(values, factor):
        return contract("bit,bij->bjt", values.reshape(blocks_here, breadth, length), factor)

    gate_sectioned = apply_right(mixed_in, gate_right)
    value_sectioned = apply_right(mixed_in, value_right)
    gate_turn = lax.all_to_all(gate_sectioned, "block", split_axis=1, concat_axis=0, tiled=True)
    value_turn = lax.all_to_all(value_sectioned, "block", split_axis=1, concat_axis=0, tiled=True)
    gate_mixed = contract("bjt,jbk->kjt", gate_turn, gate_left)
    value_mixed = contract("bjt,jbk->kjt", value_turn, value_left)
    gate_home, value_home = (
        lax.all_to_all(gate_mixed, "block", split_axis=0, concat_axis=1, tiled=True),
        lax.all_to_all(value_mixed, "block", split_axis=0, concat_axis=1, tiled=True),
    )
    hidden = gated(gate_home, value_home).reshape(channels, length)
    output_sectioned = apply_right(hidden, output_right)
    output_turn = lax.all_to_all(output_sectioned, "block", split_axis=1, concat_axis=0, tiled=True)
    output_mixed = contract("bjt,jbk->kjt", output_turn, output_left)
    output_home = lax.all_to_all(output_mixed, "block", split_axis=0, concat_axis=1, tiled=True)
    layer_out = mixed_in + output_home.reshape(channels, length)
    upstream_across = lax.all_to_all(
        upstream.reshape(blocks_here, breadth, length),
        "block",
        split_axis=1,
        concat_axis=0,
        tiled=True,
    )
    grad_output_left = contract("bjt,kjt->jbk", output_turn, upstream_across)
    sectioned_back = contract("jbk,kjt->bjt", output_left, upstream_across)
    sectioned_home = lax.all_to_all(
        sectioned_back, "block", split_axis=0, concat_axis=1, tiled=True
    )
    hidden_blocks = hidden.reshape(blocks_here, breadth, length)
    grad_output_right = contract("bit,bjt->bij", hidden_blocks, sectioned_home)
    hidden_back = contract("bij,bjt->bit", output_right, sectioned_home)
    pullback = jax.vjp(gated, gate_home, value_home)[1]
    gate_back, value_back = pullback(hidden_back)
    gate_cot, value_cot = (
        lax.all_to_all(gate_back, "block", split_axis=1, concat_axis=0, tiled=True),
        lax.all_to_all(value_back, "block", split_axis=1, concat_axis=0, tiled=True),
    )
    grad_gate_left = contract("bjt,kjt->jbk", gate_turn, gate_cot)
    grad_value_left = contract("bjt,kjt->jbk", value_turn, value_cot)
    gate_sectioned_back = contract("jbk,kjt->bjt", gate_left, gate_cot)
    value_sectioned_back = contract("jbk,kjt->bjt", value_left, value_cot)
    gate_home_back, value_home_back = (
        lax.all_to_all(gate_sectioned_back, "block", split_axis=0, concat_axis=1, tiled=True),
        lax.all_to_all(value_sectioned_back, "block", split_axis=0, concat_axis=1, tiled=True),
    )
    input_blocks = mixed_in.reshape(blocks_here, breadth, length)
    grad_gate_right = contract("bit,bjt->bij", input_blocks, gate_home_back)
    grad_value_right = contract("bit,bjt->bij", input_blocks, value_home_back)
    through_pair = contract("bij,bjt->bit", gate_right, gate_home_back) + contract(
        "bij,bjt->bit", value_right, value_home_back
    )
    mixed_back = upstream + through_pair.reshape(channels, length)
    grad_gain_part = jnp.sum(mixed_back * seq_mixed, axis=1)
    seq_back = (seq_gain[:, None] * mixed_back).reshape(channels, seq_here, seq_block)
    back_across = lax.all_to_all(seq_back, ("dp", "seq"), split_axis=2, concat_axis=1, tiled=True)
    left_part = contract("caj,cbj->jab", portion, back_across)
    sectioned_back_across = contract("jab,cbj->caj", seq_left, back_across)
    sectioned_seq_back = lax.all_to_all(
        sectioned_back_across, ("dp", "seq"), split_axis=1, concat_axis=2, tiled=True
    )
    right_part = contract("cai,caj->aij", seq_source, sectioned_seq_back)
    grad_inputs = mixed_back + contract("aij,caj->cai", seq_right, sectioned_seq_back).reshape(
        channels, length
    )
    summed = lax.psum(
        (
            grad_gate_right,
            grad_gate_left,
            grad_value_right,
            grad_value_left,
            grad_output_right,
            grad_output_left,
            grad_gain_part,
        ),
        ("dp", "seq"),
    )
    right_sum, left_sum = lax.psum((right_part, left_part), "block")
    grad_scale = 1.0 / math.sqrt(lax.axis_size("dp") * lax.axis_size("seq") * length)
    return (
        layer_out.reshape(inputs.shape),
        grad_inputs.reshape(inputs.shape),
        right_sum * grad_scale,
        left_sum * grad_scale,
        summed[6] * grad_scale,
        summed[0] * grad_scale,
        summed[1] * grad_scale,
        summed[2] * grad_scale,
        summed[3] * grad_scale,
        summed[4] * grad_scale,
        summed[5] * grad_scale,
    )


def solution(mesh):
    in_specs = (
        P("block", "groups", ("dp", "seq")),
        P("block", "groups", ("dp", "seq")),
        P(("dp", "seq"), None, None),
        P(("dp", "seq"), None, None),
        P("block"),
        P("block", None, None),
        P("block", None, None),
        P("block", None, None),
        P("block", None, None),
        P("block", None, None),
        P("block", None, None),
    )
    out_specs = (
        P("block", "groups", ("dp", "seq")),
        P("block", "groups", ("dp", "seq")),
        P(("groups", "dp", "seq"), None, None),
        P(("groups", "dp", "seq"), None, None),
        P(("groups", "block")),
        P(("groups", "block"), None, None),
        P(("groups", "block"), None, None),
        P(("groups", "block"), None, None),
        P(("groups", "block"), None, None),
        P(("groups", "block"), None, None),
        P(("groups", "block"), None, None),
    )
    return jax.shard_map(body, mesh=mesh, in_specs=in_specs, out_specs=out_specs, check_vma=False)
```

profile of v0, /device:TPU:0, one launch (start us, length us, event | category | flops | bytes accessed | tf_op | source)
XLA Modules:
  0.0 595.2 jit_solution(3259985963258901631)
XLA Ops:
  8.0 2.4 convolution_bitcast_fusion.12
  12.1 4.2 all-to-all-start
  17.2 13.6 %all-to-all-done = f32[512,4,128]{0,1,2:T(4,128)S(1)} async-done(((f32[512,4,128]{0,1,2:T(4,128)}), f32[512,4,128]{0,1,2:T(4,128)S(1)}, u32[]{:S(2)}, u32[]{:S(2)}) %all-to-all-start) | async-done | bytes 1048608 | tf_op jit(solution)/shard_map/all_to_all | solution.py:42
  34.6 3.6 all-to-all-start.1
  39.9 11.6 %all-to-all-done.1 = f32[512,8,64]{0,2,1:T(8,128)S(1)} async-done(((f32[512,8,64]{0,2,1:T(8,128)}), f32[512,8,64]{0,2,1:T(8,128)S(1)}, u32[]{:S(2)}, u32[]{:S(2)}) %all-to-all-start.1) | async-done | bytes 1048608 | tf_op jit(solution)/shard_map/all_to_all | solution.py:44
  51.5 4.8 all-to-all-start.8
  57.4 2.4 copy.260
  59.7 4.1 reshape.111
  68.3 14.7 %all-to-all-done.8 = f32[8,64,512]{2,0,1:T(8,128)} async-done(((f32[8,64,512]{2,0,1:T(8,128)}), f32[8,64,512]{2,0,1:T(8,128)}, u32[]{:S(2)}, u32[]{:S(2)}) %all-to-all-start.8) | async-done | bytes 1048608 | tf_op jit(solution)/shard_map/all_to_all | solution.py:68
  83.0 4.2 all-to-all-start.2
  90.8 23.0 %all-to-all-done.2 = f32[8,64,512]{2,0,1:T(8,128)} async-done(((f32[8,64,512]{2,0,1:T(8,128)}), f32[8,64,512]{2,0,1:T(8,128)}, u32[]{:S(2)}, u32[]{:S(2)}) %all-to-all-start.2) | async-done | bytes 1048608 | tf_op jit(solution)/shard_map/all_to_all | solution.py:54
  113.8 4.7 all-to-all-start.4
  118.5 2.3 convolution_bitcast_fusion.4
  122.4 22.7 %all-to-all-done.4 = f32[8,64,512]{2,0,1:T(8,128)} async-done(((f32[8,64,512]{2,0,1:T(8,128)}), f32[8,64,512]{2,0,1:T(8,128)}, u32[]{:S(2)}, u32[]{:S(2)}) %all-to-all-start.4) | async-done | bytes 1048608 | tf_op jit(solution)/shard_map/all_to_all | solution.py:55
  145.1 4.2 all-to-all-start.9
  149.4 2.3 convolution_bitcast_fusion.9
  153.3 22.7 %all-to-all-done.9 = f32[64,8,512]{2,1,0:T(8,128)} async-done(((f32[64,8,512]{2,1,0:T(8,128)}), f32[64,8,512]{2,1,0:T(8,128)}, u32[]{:S(2)}, u32[]{:S(2)}) %all-to-all-start.9) | async-done | bytes 1048608 | tf_op jit(solution)/shard_map/all_to_all | solution.py:77
  176.0 4.2 all-to-all-start.3
  180.2 2.3 convolution_bitcast_fusion.7
  184.1 22.7 %all-to-all-done.3 = f32[64,8,512]{2,1,0:T(8,128)} async-done(((f32[64,8,512]{2,1,0:T(8,128)}), f32[64,8,512]{2,1,0:T(8,128)}, u32[]{:S(2)}, u32[]{:S(2)}) %all-to-all-start.3) | async-done | bytes 1048608 | tf_op jit(solution)/shard_map/all_to_all | solution.py:59
  206.8 30.1 %all_to_all.282 = f32[64,8,512]{2,1,0:T(8,128)S(1)} all-to-all(f32[64,8,512]{2,1,0:T(8,128)} %copy.211), channel_id=1, replica_groups=mesh['groups'=2,'block'=8,'dp'=1,'seq'=2] {'block'}, dimensions={0} | all-to-all | bytes 2097152 | tf_op jit(solution)/shard_map/all_to_all | solution.py:60
  236.9 4.6 fusion.56
  243.1 4.2 all-to-all-start.12
  247.4 2.8 copy.225
  250.2 23.8 %all-to-all-done.12 = f32[8,64,512]{2,0,1:T(8,128)} async-done(((f32[8,64,512]{2,0,1:T(8,128)}), f32[8,64,512]{2,0,1:T(8,128)}, u32[]{:S(2)}, u32[]{:S(2)}) %all-to-all-start.12) | async-done | bytes 1048608 | tf_op jit(solution)/shard_map/all_to_all | solution.py:87
  274.0 4.2 all-to-all-start.10
  278.2 2.9 convolution_bitcast_fusion.6
  282.8 22.0 %all-to-all-done.10 = f32[8,64,512]{2,0,1:T(8,128)} async-done(((f32[8,64,512]{2,0,1:T(8,128)}), f32[8,64,512]{2,0,1:T(8,128)}, u32[]{:S(2)}, u32[]{:S(2)}) %all-to-all-start.10) | async-done | bytes 1048608 | tf_op jit(solution)/shard_map/all_to_all | solution.py:86
  304.8 4.4 all-to-all-start.6
  309.2 2.3 convolution_bitcast_fusion.1
  313.1 22.7 %all-to-all-done.6 = f32[8,64,512]{2,0,1:T(8,128)} async-done(((f32[8,64,512]{2,0,1:T(8,128)}), f32[8,64,512]{2,0,1:T(8,128)}, u32[]{:S(2)}, u32[]{:S(2)}) %all-to-all-start.6) | async-done | bytes 1048608 | tf_op jit(solution)/shard_map/all_to_all | solution.py:64
  335.8 4.2 all-to-all-start.13
  340.1 2.3 convolution_bitcast_fusion.2
  343.9 22.7 %all-to-all-done.13 = f32[64,8,512]{2,1,0:T(8,128)} async-done(((f32[64,8,512]{2,1,0:T(8,128)}), f32[64,8,512]{2,1,0:T(8,128)}, u32[]{:S(2)}, u32[]{:S(2)}) %all-to-all-start.13) | async-done | bytes 1048608 | tf_op jit(solution)/shard_map/all_to_all | solution.py:95
  366.7 4.2 all-to-all-start.11
  370.9 3.6 copy.234
  374.5 2.4 copy.198
  378.6 3.7 fusion.9
  382.3 2.3 convolution_bitcast_fusion.5
  386.2 11.3 %all-to-all-done.11 = f32[64,8,512]{2,1,0:T(8,128)} async-done(((f32[64,8,512]{2,1,0:T(8,128)}), f32[64,8,512]{2,1,0:T(8,128)}, u32[]{:S(2)}, u32[]{:S(2)}) %all-to-all-start.11) | async-done | bytes 1048608 | tf_op jit(solution)/shard_map/all_to_all | solution.py:94
  397.5 4.5 all-to-all-start.7
  402.0 3.3 fusion.12
  405.3 3.4 fusion.20
  408.7 3.4 fusion.6
  412.0 2.3 fusion.27
  414.3 3.2 convolution_add_fusion
  417.6 2.5 reshape.107
  420.1 2.5 copy.235
  426.1 3.0 fusion.17
  429.1 4.4 all-to-all-start.14
  433.8 2.3 copy.218
  436.1 2.5 copy.219
  438.6 3.2 add_add_fusion
  441.8 3.0 fusion.25
  444.8 3.7 reshape.112
  448.5 3.9 copy.248
  452.4 3.7 copy.249
  457.5 4.9 psum.65
  468.5 4.4 all-to-all-start.15
  475.0 31.4 %psum.64 = f32[64,8,8]{2,1,0:T(8,128)S(1)} all-reduce(f32[64,8,8]{2,1,0:T(8,128)S(1)} %fusion.58), channel_id=1, replica_groups=mesh['groups'=2,'block'=8,'dp'=1,'seq'=2] {'block'}, use_global_device_ids=true, to_apply=%region_1.0 | all-reduce | flops 4096 | bytes 32768 | tf_op jit(solution)/shard_map/psum | solution.py:128
  507.2 11.0 %all-reduce.6.cloned.1.call-done = (f32[8,64,64]{2,1,0:T(8,128)}, f32[8,64,64]{2,1,0:T(8,128)}, f32[8,64,64]{2,1,0:T(8,128)}, f32[8,64,64]{2,1,0:T(8,128)}, f32[8,64,64]{2,1,0:T(8,128)}, /*index=5*/f32[8,64,64]{2,1,0:T(8,128)}) async-done(((f32[8,64,64]{2,1,0:T(8,128)}, f32[8,64,64]{2,1,0:T(8,128)}, f32[8,64,64]{2,1,0:T(8,128)}, f32[8,64,64]{2,1,0:T(8,128)}, f32[8,64,64]{2,1,0:T(8,128)}, ...) | async-done | bytes 786448 | tf_op jit(solution)/shard_map/psum | solution.py:116
  528.1 2.4 copy.243
  530.5 2.8 fusion.35
  533.3 52.1 %all-reduce.4.cloned.1.call-done = f32[4,128,128]{1,2,0:T(8,128)} async-done(((f32[4,128,128]{1,2,0:T(8,128)}), f32[4,128,128]{1,2,0:T(8,128)}) %all-reduce.4.cloned.1.call-update) | async-done | bytes 262160 | tf_op jit(solution)/shard_map/psum | solution.py:128
  (99 shorter events, 57.1 us)
Async XLA Ops:
  8.0 228.9 %copy-start = (f32[8,64,64]{2,1,0:T(8,128)S(1)}, f32[8,64,64]{2,1,0:T(8,128)}, u32[]{:S(2)}) copy-start(f32[8,64,64]{2,1,0:T(8,128)} %param.20) | copy-start | bytes 393220
  10.4 5.9 copy-start.22
  12.1 18.6 %all-to-all-start = ((f32[512,4,128]{0,1,2:T(4,128)}), f32[512,4,128]{0,1,2:T(4,128)S(1)}, u32[]{:S(2)}, u32[]{:S(2)}) async-start(f32[512,4,128]{0,1,2:T(4,128)} %copy.193), calls=%async_computation | async-start | bytes 2097152 | tf_op jit(solution)/shard_map/all_to_all | solution.py:42
  30.9 1.0 copy-start.9
  31.9 2.7 copy-start.4
  33.0 5.2 copy-start.6
  34.6 16.9 %all-to-all-start.1 = ((f32[512,8,64]{0,2,1:T(8,128)}), f32[512,8,64]{0,2,1:T(8,128)S(1)}, u32[]{:S(2)}, u32[]{:S(2)}) async-start(f32[512,8,64]{0,2,1:T(8,128)} %copy.196), calls=%async_computation.1 | async-start | bytes 2097152 | tf_op jit(solution)/shard_map/all_to_all | solution.py:44
  38.3 18.0 %copy-start.2 = (f32[512,1,512]{2,1,0:T(1,128)S(1)}, f32[512,1,512]{2,1,0:T(1,128)}, u32[]{:S(2)}) copy-start(f32[512,1,512]{2,1,0:T(1,128)} %param.11) | copy-start | bytes 3145732
  39.9 17.4 %copy-start.23 = (f32[512]{0:T(512)S(1)}, f32[512]{0:T(512)}, u32[]{:S(2)}) copy-start(f32[512]{0:T(512)} %param.15) | copy-start | bytes 6148
  51.5 31.5 %all-to-all-start.8 = ((f32[8,64,512]{2,0,1:T(8,128)}), f32[8,64,512]{2,0,1:T(8,128)}, u32[]{:S(2)}, u32[]{:S(2)}) async-start(f32[8,64,512]{2,0,1:T(8,128)} %copy.220), calls=%async_computation.8 | async-start | bytes 2097152 | tf_op jit(solution)/shard_map/all_to_all | solution.py:68
  63.8 1.8 copy-start.14
  83.0 30.8 %all-to-all-start.2 = ((f32[8,64,512]{2,0,1:T(8,128)}), f32[8,64,512]{2,0,1:T(8,128)}, u32[]{:S(2)}, u32[]{:S(2)}) async-start(f32[8,64,512]{2,0,1:T(8,128)} %copy.202), calls=%async_computation.2 | async-start | bytes 2097152 | tf_op jit(solution)/shard_map/all_to_all | solution.py:54
  113.8 31.3 %all-to-all-start.4 = ((f32[8,64,512]{2,0,1:T(8,128)}), f32[8,64,512]{2,0,1:T(8,128)}, u32[]{:S(2)}, u32[]{:S(2)}) async-start(f32[8,64,512]{2,0,1:T(8,128)} %copy.208), calls=%async_computation.4 | async-start | bytes 2097152 | tf_op jit(solution)/shard_map/all_to_all | solution.py:55
  145.1 30.8 %all-to-all-start.9 = ((f32[64,8,512]{2,1,0:T(8,128)}), f32[64,8,512]{2,1,0:T(8,128)}, u32[]{:S(2)}, u32[]{:S(2)}) async-start(f32[64,8,512]{2,1,0:T(8,128)} %copy.223), calls=%async_computation.9 | async-start | bytes 2097152 | tf_op jit(solution)/shard_map/all_to_all | solution.py:77
  176.0 30.8 %all-to-all-start.3 = ((f32[64,8,512]{2,1,0:T(8,128)}), f32[64,8,512]{2,1,0:T(8,128)}, u32[]{:S(2)}, u32[]{:S(2)}) async-start(f32[64,8,512]{2,1,0:T(8,128)} %copy.205), calls=%async_computation.3 | async-start | bytes 2097152 | tf_op jit(solution)/shard_map/all_to_all | solution.py:59
  236.9 4.6 copy-start.17
  243.1 30.8 %all-to-all-start.12 = ((f32[8,64,512]{2,0,1:T(8,128)}), f32[8,64,512]{2,0,1:T(8,128)}, u32[]{:S(2)}, u32[]{:S(2)}) async-start(f32[8,64,512]{2,0,1:T(8,128)} %copy.229), calls=%async_computation.12 | async-start | bytes 2097152 | tf_op jit(solution)/shard_map/all_to_all | solution.py:87
  274.0 30.8 %all-to-all-start.10 = ((f32[8,64,512]{2,0,1:T(8,128)}), f32[8,64,512]{2,0,1:T(8,128)}, u32[]{:S(2)}, u32[]{:S(2)}) async-start(f32[8,64,512]{2,0,1:T(8,128)} %copy.225), calls=%async_computation.10 | async-start | bytes 2097152 | tf_op jit(solution)/shard_map/all_to_all | solution.py:86
  281.2 28.1 %copy-start.11 = (f32[8,64,64]{2,1,0:T(8,128)S(1)}, f32[8,64,64]{2,1,0:T(8,128)}, u32[]{:S(2)}) copy-start(f32[8,64,64]{2,1,0:T(8,128)} %param.19) | copy-start | bytes 393220
  304.8 31.0 %all-to-all-start.6 = ((f32[8,64,512]{2,0,1:T(8,128)}), f32[8,64,512]{2,0,1:T(8,128)}, u32[]{:S(2)}, u32[]{:S(2)}) async-start(f32[8,64,512]{2,0,1:T(8,128)} %copy.214), calls=%async_computation.6 | async-start | bytes 2097152 | tf_op jit(solution)/shard_map/all_to_all | solution.py:64
  311.5 28.6 %copy-start.12 = (f32[8,64,64]{2,1,0:T(8,128)S(1)}, f32[8,64,64]{2,1,0:T(8,128)}, u32[]{:S(2)}) copy-start(f32[8,64,64]{2,1,0:T(8,128)} %param.17) | copy-start | bytes 393220
  335.8 30.8 %all-to-all-start.13 = ((f32[64,8,512]{2,1,0:T(8,128)}), f32[64,8,512]{2,1,0:T(8,128)}, u32[]{:S(2)}, u32[]{:S(2)}) async-start(f32[64,8,512]{2,1,0:T(8,128)} %copy.231), calls=%async_computation.13 | async-start | bytes 2097152 | tf_op jit(solution)/shard_map/all_to_all | solution.py:95
  366.7 30.8 %all-to-all-start.11 = ((f32[64,8,512]{2,1,0:T(8,128)}), f32[64,8,512]{2,1,0:T(8,128)}, u32[]{:S(2)}, u32[]{:S(2)}) async-start(f32[64,8,512]{2,1,0:T(8,128)} %copy.227), calls=%async_computation.11 | async-start | bytes 2097152 | tf_op jit(solution)/shard_map/all_to_all | solution.py:94
  377.0 1.6 copy-start.18
  378.6 3.7 copy-start.13
  397.5 31.6 %all-to-all-start.7 = ((f32[64,8,512]{2,1,0:T(8,128)}), f32[64,8,512]{2,1,0:T(8,128)}, u32[]{:S(2)}, u32[]{:S(2)}) async-start(f32[64,8,512]{2,1,0:T(8,128)} %copy.217), calls=%async_computation.7 | async-start | bytes 2097152 | tf_op jit(solution)/shard_map/all_to_all | solution.py:66
  405.3 6.7 %copy-start.15 = (f32[8,64,64]{2,1,0:T(8,128)S(1)}, f32[8,64,64]{2,1,0:T(8,128)}, u32[]{:S(2)}) copy-start(f32[8,64,64]{2,1,0:T(8,128)} %param.16) | copy-start | bytes 393220
  408.7 5.6 copy-start.19
  429.1 34.0 %all-to-all-start.14 = ((f32[512,4,128]{0,1,2:T(4,128)}), f32[512,4,128]{0,1,2:T(4,128)}, u32[]{:S(2)}, u32[]{:S(2)}) async-start(f32[512,4,128]{0,1,2:T(4,128)} %copy.236), calls=%async_computation.14 | async-start | bytes 2097152 | tf_op jit(solution)/shard_map/all_to_all | solution.py:106
  433.5 84.7 %all-reduce.6.cloned.1.call-start = ((), (), s32[]{:S(2)}) async-start(), calls=%async_computation.17 | async-start | bytes 3145728 | tf_op jit(solution)/shard_map/psum | solution.py:116
  452.4 3.7 copy-start.8
  464.9 1.1 copy-start.10
  466.9 6.1 %copy-start.5 = (f32[512,8,64]{0,1,2:T(8,128)S(1)}, f32[512,8,64]{0,1,2:T(8,128)}, u32[]{:S(2)}) copy-start(f32[512,8,64]{0,1,2:T(8,128)} %copy-done.4) | copy-start | bytes 3145732
  468.5 54.3 %all-to-all-start.15 = ((f32[512,8,64]{0,2,1:T(8,128)}), f32[512,8,64]{0,2,1:T(8,128)}, u32[]{:S(2)}, u32[]{:S(2)}) async-start(f32[512,8,64]{0,2,1:T(8,128)} %copy.240), calls=%async_computation.15 | async-start | bytes 2097152 | tf_op jit(solution)/shard_map/all_to_all | solution.py:109
  473.0 112.5 %all-reduce.4.cloned.1.call-start = ((), (), s32[]{:S(2)}) async-start(), calls=%async_computation.16 | async-start | bytes 524288 | tf_op jit(solution)/shard_map/psum | solution.py:128
  518.2 3.8 copy-start.20
  518.2 3.8 copy-start.21
  520.1 4.1 copy-start.16
  526.2 4.3 copy-start.3
  526.2 4.3 copy-start.7
  530.5 56.7 %copy-start.1 = (f32[8,64,64]{2,1,0:T(8,128)S(1)}, f32[8,64,64]{2,1,0:T(8,128)}, u32[]{:S(2)}) copy-start(f32[8,64,64]{2,1,0:T(8,128)} %param.20) | copy-start | bytes 393220
Sparse Core Ops, SparseCore 0:
  456.2 61.9 all-reduce.5
Sparse Core Ops, SparseCore 1:
  530.6 54.8 all-reduce.3
where the time goes:
time: 606 us; the launch traced here: 595 us
  waiting for transfers between devices  297 us (49%)
  local copies, waits for them, and re-layouts  73.4 us (12%)
  blocking collectives  66.4 us (11%)
  starting transfers between devices  65.1 us (11%)
  matrix products  60 us (10%)
  other arithmetic  17.1 us (3%)
  between operations  16.5 us (3%)
    dot_general x24, matrix products, contract(): return jnp.einsum(pattern, former, latter, precision=precise)  60 us
    psum x1, waiting for transfers between devices, body(): right_sum, left_sum = lax.psum((right_part, left_part), 'block')  52.1 us
    psum x1, blocking collectives, body(): right_sum, left_sum = lax.psum((right_part, left_part), 'block')  31.4 us
    all_to_all x1, blocking collectives, body(): lax.all_to_all(value_mixed, 'block', split_axis=0, concat_axis=1, tiled=T...  30.1 us
    all_to_all x1, waiting for transfers between devices, body(): lax.all_to_all(value_back, 'block', split_axis=1, concat_axis=0, tiled=True)  23.8 us
    all_to_all x1, waiting for transfers between devices, body(): lax.all_to_all(gate_sectioned, 'block', split_axis=1, concat_axis=0, tile...  23 us
    all_to_all x1, waiting for transfers between devices, body(): lax.all_to_all(value_sectioned_back, 'block', split_axis=0, concat_axis=1...  22.7 us
    all_to_all x1, waiting for transfers between devices, body(): lax.all_to_all(sectioned_back, 'block', split_axis=0, concat_axis=1, tile...  22.7 us
  transfers between devices with their start and end apart: 17, of which 14 were waited for; matrix products, arithmetic and copies ran while one was open for 21% of the time, Pallas kernels for 0%

commit v1 on v0

v1 whole, which is shorter than its diff:
```python
import math

import jax
import jax.numpy as jnp
from jax import lax
from jax.sharding import PartitionSpec as P

LANES = 128
ROWS = ("dp", "seq")
EVERY = ("dp", "seq", "block")


def contract(pattern, former, latter):
    return jnp.einsum(
        pattern, former, latter, precision=lax.Precision.HIGH, preferred_element_type=jnp.float32
    )


def gated(gate_in, value_in):
    return jax.nn.gelu(gate_in) * value_in


def pack(pieces):
    parts, channels, tokens = pieces.shape
    fold = max(1, LANES // tokens)
    folded = pieces.reshape(parts, fold, channels // fold, tokens).transpose(0, 2, 1, 3)
    return folded.reshape(parts, channels // fold, fold * tokens)


def unpack(rows, tokens):
    parts, count, width = rows.shape
    fold = width // tokens
    return rows.reshape(parts, count, fold, tokens).transpose(0, 2, 1, 3).reshape(parts, count * fold, tokens)


def trade(rows, axes):
    return lax.all_to_all(rows, axes, split_axis=0, concat_axis=0, tiled=True)


def body(
    inputs,
    cotangent,
    seq_right,
    seq_left,
    seq_gain,
    gate_right,
    gate_left,
    value_right,
    value_left,
    output_right,
    output_left,
):
    channels = inputs.shape[0]
    length = inputs.shape[1] * inputs.shape[2]
    row_count = lax.axis_size("dp") * lax.axis_size("seq")
    block_count = lax.axis_size("block")
    row_index = lax.axis_index("dp") * lax.axis_size("seq") + lax.axis_index("seq")
    block_index = lax.axis_index("block")
    everyone = row_count * block_count
    source = inputs.reshape(channels, length)
    upstream = cotangent.reshape(channels, length)
    blocks_here = gate_right.shape[0]
    breadth = gate_right.shape[1]
    blocks = blocks_here * block_count
    seq_block = seq_right.shape[1]
    seq_count = seq_right.shape[0] * row_count
    width = blocks * breadth
    mine = channels // row_count
    total = length * row_count
    tokens = length // block_count

    stacked = jnp.concatenate(
        [
            jnp.concatenate([gate_right, value_right], axis=2)[:, None],
            jnp.concatenate([gate_left, value_left], axis=2)[:, None],
            jnp.concatenate([output_right, output_left], axis=2)[:, None],
        ],
        axis=1,
    )
    factors = lax.all_gather(stacked, "block", axis=0, tiled=True)
    right_pair = factors[:, 0]
    gate_l, value_l = factors[:, 1, :, :breadth], factors[:, 1, :, breadth:]
    out_r, out_l = factors[:, 2, :, :breadth], factors[:, 2, :, breadth:]
    right_all = lax.all_gather(seq_right, ROWS, axis=0, tiled=True)
    left_turned = lax.all_gather(seq_left.transpose(1, 2, 0), ROWS, axis=2, tiled=True)

    def to_channels(values):
        arrived = trade(values.reshape(row_count, mine, length), ROWS)
        return arrived.transpose(1, 0, 2).reshape(mine, total)

    own = to_channels(source)
    own_blocks = own.reshape(mine, seq_count, seq_block)
    sectioned_seq = contract("cai,aij->caj", own_blocks, right_all)
    seq_mixed = jnp.sum(left_turned[None] * sectioned_seq[:, :, None, :], axis=1)
    gain = lax.dynamic_slice_in_dim(seq_gain, row_index * mine, mine)
    mixed_own = own + gain[:, None] * seq_mixed.reshape(mine, total)

    def to_tokens(values):
        pieces = values.reshape(mine, everyone, tokens).transpose(1, 0, 2)
        arrived = unpack(trade(pack(pieces), EVERY), tokens)
        return (
            arrived.reshape(row_count, block_count, mine, tokens)
            .transpose(1, 0, 2, 3)
            .reshape(blocks, breadth, tokens)
        )

    across = upstream.reshape(channels, block_count, tokens).transpose(1, 0, 2)
    up = unpack(trade(pack(across), "block"), tokens).reshape(blocks, breadth, tokens)
    mixed = to_tokens(mixed_own)

    pair = contract("bit,bij->bjt", mixed, right_pair)
    gate_s, value_s = pair[:, :breadth], pair[:, breadth:]
    gate_mixed = contract("bjt,jbk->kjt", gate_s, gate_l)
    value_mixed = contract("bjt,jbk->kjt", value_s, value_l)
    hidden, pullback = jax.vjp(gated, gate_mixed, value_mixed)
    output_s = contract("bit,bij->bjt", hidden, out_r)
    layer = mixed + contract("bjt,jbk->kjt", output_s, out_l)

    def to_home(values):
        pieces = values.reshape(block_count, channels, tokens)
        arrived = unpack(trade(pack(pieces), "block"), tokens)
        return arrived.transpose(1, 0, 2).reshape(channels, length)

    layer_out = to_home(layer)

    grad_out_l = contract("bjt,kjt->jbk", output_s, up)
    output_back = contract("jbk,kjt->bjt", out_l, up)
    grad_out_r = contract("bit,bjt->bij", hidden, output_back)
    hidden_back = contract("bij,bjt->bit", out_r, output_back)
    gate_back, value_back = pullback(hidden_back)
    grad_gate_l = contract("bjt,kjt->jbk", gate_s, gate_back)
    grad_value_l = contract("bjt,kjt->jbk", value_s, value_back)
    pair_back = jnp.concatenate(
        [contract("jbk,kjt->bjt", gate_l, gate_back), contract("jbk,kjt->bjt", value_l, value_back)],
        axis=1,
    )
    grad_right_pair = contract("bit,bjt->bij", mixed, pair_back)
    mixed_back = up + contract("bij,bjt->bit", right_pair, pair_back)

    grad_scale = 1.0 / math.sqrt(total)
    grads = jnp.concatenate(
        [
            grad_right_pair[:, None],
            jnp.concatenate([grad_gate_l, grad_value_l], axis=2)[:, None],
            jnp.concatenate([grad_out_r, grad_out_l], axis=2)[:, None],
        ],
        axis=1,
    )
    grads = lax.psum_scatter(grads * grad_scale, "block", scatter_dimension=0, tiled=True)
    grads = lax.psum(grads, ROWS)

    pieces = (
        mixed_back.reshape(block_count, row_count, mine, tokens)
        .transpose(1, 0, 2, 3)
        .reshape(everyone, mine, tokens)
    )
    back_own = unpack(trade(pack(pieces), EVERY), tokens).transpose(1, 0, 2).reshape(mine, total)
    gain_part = jnp.sum(back_own * seq_mixed.reshape(mine, total), axis=1)
    seq_back = (gain[:, None] * back_own).reshape(mine, seq_count, seq_block)
    left_part = jnp.sum(sectioned_seq[:, :, None, :] * seq_back[:, None, :, :], axis=0)
    sectioned_back = jnp.sum(left_turned[None] * seq_back[:, None, :, :], axis=2)
    right_part = contract("cai,caj->aij", own_blocks, sectioned_back)
    grad_own = back_own + contract("aij,caj->cai", right_all, sectioned_back).reshape(mine, total)
    grad_inputs = trade(
        grad_own.reshape(mine, row_count, length).transpose(1, 0, 2), ROWS
    ).reshape(channels, length)

    gain_row = lax.dynamic_update_slice_in_dim(
        jnp.zeros((width,), jnp.float32), gain_part, block_index * channels + row_index * mine, 0
    )
    tail = jnp.concatenate(
        [
            right_part.reshape(-1, LANES),
            left_part.reshape(-1, LANES),
            gain_row.reshape(-1, LANES),
        ],
        axis=0,
    )
    tail = lax.psum(tail * grad_scale, EVERY)
    right_rows = right_part.size // LANES
    left_rows = left_part.size // LANES
    right_sum = lax.dynamic_slice_in_dim(
        tail[:right_rows].reshape(right_part.shape), row_index * seq_right.shape[0], seq_right.shape[0]
    )
    left_sum = lax.dynamic_slice_in_dim(
        tail[right_rows : right_rows + left_rows].reshape(left_part.shape),
        row_index * seq_left.shape[0],
        seq_left.shape[0],
        axis=2,
    ).transpose(2, 0, 1)
    gain_sum = lax.dynamic_slice_in_dim(
        tail[right_rows + left_rows :].reshape(-1), block_index * channels, channels
    )
    return (
        layer_out.reshape(inputs.shape),
        grad_inputs.reshape(inputs.shape),
        right_sum,
        left_sum,
        gain_sum,
        grads[:, 0, :, :breadth],
        grads[:, 1, :, :breadth],
        grads[:, 0, :, breadth:],
        grads[:, 1, :, breadth:],
        grads[:, 2, :, :breadth],
        grads[:, 2, :, breadth:],
    )


def solution(mesh):
    in_specs = (
        P("block", "groups", ("dp", "seq")),
        P("block", "groups", ("dp", "seq")),
        P(("dp", "seq"), None, None),
        P(("dp", "seq"), None, None),
        P("block"),
        P("block", None, None),
        P("block", None, None),
        P("block", None, None),
        P("block", None, None),
        P("block", None, None),
        P("block", None, None),
    )
    out_specs = (
        P("block", "groups", ("dp", "seq")),
        P("block", "groups", ("dp", "seq")),
        P(("groups", "dp", "seq"), None, None),
        P(("groups", "dp", "seq"), None, None),
        P(("groups", "block")),
        P(("groups", "block"), None, None),
        P(("groups", "block"), None, None),
        P(("groups", "block"), None, None),
        P(("groups", "block"), None, None),
        P(("groups", "block"), None, None),
        P(("groups", "block"), None, None),
    )
    return jax.shard_map(body, mesh=mesh, in_specs=in_specs, out_specs=out_specs, check_vma=False)
```

time: 606 us -> 470 us (0.78)
  waiting for transfers between devices: 297 us -> 230 us
  blocking collectives: 66.4 us -> 18.1 us
  starting transfers between devices: 65.1 us -> 25.5 us
  local copies, waits for them, and re-layouts: 73.4 us -> 91.6 us
    all_to_all x15 -> x6, waiting for transfers between devices: 234 us -> 119 us  [trade(): return lax.all_to_all(rows, axes, split_axis=0, concat_axis=0, tiled=True)]
    psum x2, waiting for transfers between devices: 63.1 us -> 111 us  [the longest x1 82.5 us: body(): tail = lax.psum(tail * grad_scale, EVERY)]
    all_to_all x15 -> x6, starting transfers between devices: 64.7 us -> 25.2 us  [trade(): return lax.all_to_all(rows, axes, split_axis=0, concat_axis=0, tiled=True)]
    psum x2 -> x0, blocking collectives: 36.4 us -> none  [the longest x1 31.4 us: body(): right_sum, left_sum = lax.psum((right_part, left_part), 'block')]
    all_to_all x1 -> x0, blocking collectives: 30.1 us -> none  [body(): lax.all_to_all(value_mixed, 'block', split_axis=0, concat_axis=1, tiled=T...]
    all_gather x0 -> x2, blocking collectives: none -> 18.1 us  [the longest x1 9.39 us: body(): lax.all_gather(seq_left.transpose(1, 2, 0), ROWS, axis=2, tiled=True)]
    another operation x1 -> x7, local copies, waits for them, and re-layouts: 1.62 us -> 14.4 us  [the longest x3 8.94 us: body(): unpack(trade(pack(across), 'block'), tokens)]
    slice x0 -> x4, local copies, waits for them, and re-layouts: none -> 11.7 us  [the longest x3 10.6 us: body(): gate_s, value_s = (pair[:, :breadth], pair[:, breadth:])]
  transfers between devices with their start and end apart: 17 -> 10, of which waited for: 14 -> 7; matrix products, arithmetic and copies ran while one was open for 21% -> 19% of each run, Pallas kernels for 0% -> 0%
where the time goes in v1:
time: 470 us; the launch traced here: 465 us
  waiting for transfers between devices  230 us (49%)
  local copies, waits for them, and re-layouts  91.6 us (19%)
  matrix products  63 us (13%)
  starting transfers between devices  25.5 us (5%)
  other arithmetic  21.7 us (5%)
  blocking collectives  18.1 us (4%)
  between operations  14.8 us (3%)
    all_to_all x6, waiting for transfers between devices, trade(): return lax.all_to_all(rows, axes, split_axis=0, concat_axis=0, tiled=True)  119 us
    psum x1, waiting for transfers between devices, body(): tail = lax.psum(tail * grad_scale, EVERY)  82.5 us
    dot_general x18, matrix products, contract(): jnp.einsum(pattern, former, latter, precision=lax.Precision.HIGH, preferr...  63 us
    psum x1, waiting for transfers between devices, body(): grads = lax.psum(grads, ROWS)  28.5 us
    all_to_all x6, starting transfers between devices, trade(): return lax.all_to_all(rows, axes, split_axis=0, concat_axis=0, tiled=True)  25.2 us
    unnamed x59, local copies, waits for them, and re-layouts  20 us
    slice x3, local copies, waits for them, and re-layouts, body(): gate_s, value_s = (pair[:, :breadth], pair[:, breadth:])  10.6 us
  transfers between devices with their start and end apart: 10, of which 7 were waited for; matrix products, arithmetic and copies ran while one was open for 19% of the time, Pallas kernels for 0%

profile of v1, /device:TPU:0, one launch (start us, length us, event | category | flops | bytes accessed | tf_op | source)
XLA Modules:
  0.0 464.6 jit_solution(3586838531994403406)
XLA Ops:
  8.4 1.5 maximum_bitcast_fusion.2
  11.9 4.2 all-to-all-start
  16.1 2.3 copy.268
  19.6 11.0 %all-to-all-done = f32[2,256,512]{2,1,0:T(8,128)S(1)} async-done(((f32[2,256,512]{2,1,0:T(8,128)}), f32[2,256,512]{2,1,0:T(8,128)S(1)}, u32[]{:S(2)}, u32[]{:S(2)}) %all-to-all-start) | async-done | bytes 1048608 | tf_op jit(solution)/shard_map/all_to_all | solution.py:37
  30.6 5.1 %all-to-all-start.3 = ((f32[8,256,128]{1,2,0:T(8,128)}), f32[8,256,128]{1,2,0:T(8,128)}, u32[]{:S(2)}, u32[]{:S(2)}) async-start(f32[8,256,128]{1,2,0:T(8,128)} %bitcast.32), calls=%async_computation.3 | async-start | bytes 2097152 | tf_op jit(solution)/shard_map/all_to_all | solution.py:37
  35.9 9.4 %all_gather.9 = f32[8,8,128]{1,0,2:T(8,128)S(1)} all-gather(f32[8,8,64]{1,0,2:T(8,128)S(1)} %bitcast.238), channel_id=1, replica_groups=mesh['groups'=2,'block'=8,'dp'=1,'seq'=2] {'dp','seq'}, dimensions={2}, use_global_device_ids=true | all-gather | bytes 49152 | tf_op jit(solution)/shard_map/all_gather | solution.py:85
  45.5 8.7 %all_gather.10 = f32[8,128,128]{2,1,0:T(8,128)S(1)} all-gather(f32[4,128,128]{2,1,0:T(8,128)S(1)} %copy-done.21), channel_id=1, replica_groups=mesh['groups'=2,'block'=8,'dp'=1,'seq'=2] {'dp','seq'}, dimensions={0}, use_global_device_ids=true | all-gather | bytes 786432 | tf_op jit(solution)/shard_map/all_gather | solution.py:84
  56.1 2.1 multiply_reduce_fusion.2
  58.2 1.6 copy.251
  59.8 1.2 copy_bitcast_fusion.3
  61.0 28.9 %all-to-all-done.3 = f32[8,256,128]{1,2,0:T(8,128)} async-done(((f32[8,256,128]{1,2,0:T(8,128)}), f32[8,256,128]{1,2,0:T(8,128)}, u32[]{:S(2)}, u32[]{:S(2)}) %all-to-all-start.3) | async-done | bytes 1048608 | tf_op jit(solution)/shard_map/all_to_all | solution.py:37
  89.9 4.3 all-to-all-start.1
  94.5 3.0 copy.270
  97.5 2.3 reshape_reshape.33
  99.8 3.1 copy.271
  102.9 17.1 %all-to-all-done.1 = f32[16,128,128]{1,2,0:T(8,128)} async-done(((f32[16,128,128]{1,2,0:T(8,128)}), f32[16,128,128]{1,2,0:T(8,128)}, u32[]{:S(2)}, u32[]{:S(2)}) %all-to-all-start.1) | async-done | bytes 1048608 | tf_op jit(solution)/shard_map/all_to_all | solution.py:37
  120.0 2.0 copy.253
  123.7 2.4 reshape.126
  126.1 2.4 copy.287
  128.5 4.1 fusion.15
  132.7 2.8 fusion.38
  135.4 3.8 copy.259
  139.2 4.1 copy.257
  143.4 4.8 %fusion.17 = f32[64,64,64]{2,1,0:T(8,128)S(1)} fusion(f32[64,64,64]{2,0,1:T(8,128)} %copy.259, f32[64,3,64,128]{3,2,0,1:T(8,128)} %all-gather.2.cloned.1.call-done), kind=kOutput, calls=%fused_computation.37 | convolution fusion | flops 100663296 | bytes 5242880 | tf_op jit(solution)/shard_map/bjt,jbk->kjt/dot_general | solution.py:14
  148.2 3.1 fusion.31
  151.3 2.3 fusion.10
  153.7 3.8 fusion.5
  157.5 4.8 %fusion.37 = f32[64,64,64]{2,1,0:T(8,128)} fusion(f32[64,64,64]{2,0,1:T(8,128)S(1)} %copy-done.7, f32[64,64,64]{2,1,0:T(8,128)S(1)} %fusion.10, f32[64,64,64]{2,1,0:T(8,128)S(1)} %get-tuple-element.78), kind=kOutput, calls=%fused_computation.80 | convolution fusion | flops 103022592 | bytes 4194304 | tf_op jit(solution)/shard_map/bjt,kjt->jbk/dot_general | solution.py:14
  162.3 3.1 fusion.39
  165.5 5.5 %fusion.18 = f32[64,64,64]{2,1,0:T(8,128)} fusion(f32[64,64,64]{2,0,1:T(8,128)S(1)} %fusion.31, f32[64,64,64]{2,0,1:T(8,128)S(1)} %get-tuple-element.69), kind=kOutput, calls=%fused_computation.39 | convolution fusion | flops 100663296 | bytes 3145728 | tf_op jit(solution)/shard_map/bit,bjt->bij/dot_general | solution.py:14
  170.9 2.9 fusion.11
  173.9 1.3 copy-done.4
  175.2 4.4 fusion.21
  179.6 3.6 fusion.26
  183.1 1.9 fusion.28
  185.0 2.6 pad_maximum_fusion
  187.6 5.6 %copy.277 = f32[64,128,64]{1,2,0:T(8,128)} copy(f32[64,128,64]{0,2,1:T(8,128)} %pad_maximum_fusion) | data formatting | bytes 4194304 | tf_op jit(solution)/shard_map/concatenate | solution.py:133
  193.3 2.9 convolution_bitcast_fusion
  199.0 1.4 maximum_multiply_fusion
  201.5 6.2 %copy.343 = f32[8,8,192,128]{3,1,2,0:T(8,128)} copy(f32[8,8,192,128]{3,2,1,0:T(8,128)S(1)} %bitcast.218) | data formatting | bytes 12582912
  207.8 4.3 copy.264
  212.1 7.3 %bitcast_add_fusion = f32[64,64,64]{2,0,1:T(8,128)} fusion(f32[64,64,64]{2,0,1:T(8,128)} %copy.264, f32[64,64,64]{2,1,0:T(8,128)S(1)} %copy-done.5, f32[64,3,64,128]{3,2,0,1:T(8,128)} %all-gather.2.cloned.1.call-done), kind=kOutput, calls=%fused_computation.21 | convolution fusion | flops 100925440 | bytes 6291456 | tf_op jit(solution)/shard_map/bjt,jbk->kjt/dot_general | solution.py:14
  219.4 3.6 copy.265
  223.0 1.9 reshape_reshape.30
  224.9 2.8 copy.266
  227.7 4.2 all-to-all-start.2
  232.0 3.5 copy.278
  235.5 5.3 %fusion.27 = f32[64,64,64]{2,1,0:T(8,128)} fusion(f32[64,64,64]{2,1,0:T(8,128)} %copy.278, f32[64,128,64]{1,2,0:T(8,128)S(1)} %copy-done.3, f32[64,3,64,128]{3,2,0,1:T(8,128)} %all-gather.2.cloned.1.call-done), kind=kOutput, calls=%fused_computation.48 | convolution fusion | flops 201588736 | bytes 7340032 | tf_op jit(solution)/shard_map/bij,bjt->bit/dot_general | solution.py:14
  240.8 2.2 copy.304
  245.3 30.5 %all-to-all-done.2 = f32[8,256,128]{1,2,0:T(8,128)} async-done(((f32[8,256,128]{1,2,0:T(8,128)}), f32[8,256,128]{1,2,0:T(8,128)}, u32[]{:S(2)}, u32[]{:S(2)}) %all-to-all-start.2) | async-done | bytes 1048608 | tf_op jit(solution)/shard_map/all_to_all | solution.py:37
  275.8 3.7 all-to-all-start.4
  279.5 1.4 copy.310
  280.9 1.9 copy.295
  282.8 31.3 %all-to-all-done.4 = f32[16,128,128]{1,2,0:T(8,128)S(1)} async-done(((f32[16,128,128]{1,2,0:T(8,128)}), f32[16,128,128]{1,2,0:T(8,128)S(1)}, u32[]{:S(2)}, u32[]{:S(2)}) %all-to-all-start.4) | async-done | bytes 1048608 | tf_op jit(solution)/shard_map/all_to_all | solution.py:37
  316.1 2.6 copy.283
  318.7 1.7 fusion.32
  320.8 4.9 %multiply_reduce_fusion = (f32[8,8,128]{2,1,0:T(8,128)S(1)}, f32[256,8,128]{2,1,0:T(8,128)S(1)}) fusion(f32[256,8,128]{2,1,0:T(8,128)} %copy.283, f32[256,8,128]{2,1,0:T(8,128)S(1)} %copy-done.9, f32[8,8,128]{2,1,0:T(8,128)S(1)} %copy.246), kind=kLoop, calls=%fused_computation | loop fusion | flops 8118272 | bytes 3211264 | tf_op jit(solution)/shard_map/reduce_sum | solution.py:160
  328.0 1.8 fusion.35
  329.8 2.2 copy.306
  333.1 3.6 all-to-all-start.5
  336.7 82.5 %all-reduce.3.cloned.1.call-done = f32[1120,128]{1,0:T(8,128)} async-done(((f32[1120,128]{1,0:T(8,128)}), f32[1120,128]{1,0:T(8,128)}) %all-reduce.3.cloned.1.call-update) | async-done | bytes 573456 | tf_op jit(solution)/shard_map/psum | solution.py:179
  424.1 2.2 reshape_reshape.35
  426.3 28.5 %all-reduce.5.cloned.1.call-done = f32[8,3,64,128]{3,2,0,1:T(8,128)} async-done(((f32[8,3,64,128]{3,2,0,1:T(8,128)}), f32[8,3,64,128]{3,2,0,1:T(8,128)}) %all-reduce.5.cloned.1.call-update) | async-done | bytes 786448 | tf_op jit(solution)/shard_map/psum | solution.py:150
  454.9 2.7 slice_bitcast_fusion.25
  (95 shorter events, 25.5 us)
Async XLA Ops:
  7.2 121.4 %all-gather.2.cloned.1.call-start = ((), (), s32[]{:S(2)}) async-start(), calls=%async_computation.7 | async-start | bytes 7077888 | tf_op jit(solution)/shard_map/all_gather | solution.py:80
  8.4 2.5 copy-start.20
  11.9 18.6 %all-to-all-start = ((f32[2,256,512]{2,1,0:T(8,128)}), f32[2,256,512]{2,1,0:T(8,128)S(1)}, u32[]{:S(2)}, u32[]{:S(2)}) async-start(f32[2,256,512]{2,1,0:T(8,128)} %bitcast.82), calls=%async_computation | async-start | bytes 2097152 | tf_op jit(solution)/shard_map/all_to_all | solution.py:37
  18.5 17.2 %copy-start.22 = (f32[64,8,8]{0,2,1:T(8,128)S(1)}, f32[64,8,8]{0,2,1:T(8,128)}, u32[]{:S(2)}) copy-start(f32[64,8,8]{0,2,1:T(8,128)} %param.14) | copy-start | bytes 49156
  19.6 25.8 %copy-start.23 = (f32[512]{0:T(512)S(1)}, f32[512]{0:T(512)}, u32[]{:S(2)}) copy-start(f32[512]{0:T(512)} %param.15) | copy-start | bytes 6148
  19.6 25.9 %copy-start.21 = (f32[4,128,128]{2,1,0:T(8,128)S(1)}, f32[4,128,128]{2,1,0:T(8,128)}, u32[]{:S(2)}) copy-start(f32[4,128,128]{2,1,0:T(8,128)} %param.13) | copy-start | bytes 786436
  30.6 59.3 %all-to-all-start.3 = ((f32[8,256,128]{1,2,0:T(8,128)}), f32[8,256,128]{1,2,0:T(8,128)}, u32[]{:S(2)}, u32[]{:S(2)}) async-start(f32[8,256,128]{1,2,0:T(8,128)} %bitcast.32), calls=%async_computation.3 | async-start | bytes 2097152 | tf_op jit(solution)/shard_map/all_to_all | solution.py:37
  54.2 0.8 copy-start.19
  56.1 3.7 copy-start.8
  59.8 30.1 %copy-start.12 = (f32[256,8,128]{0,2,1:T(8,128)}, f32[256,8,128]{0,2,1:T(8,128)S(1)}, u32[]{:S(2)}) copy-start(f32[256,8,128]{0,2,1:T(8,128)S(1)} %copy.251) | copy-start | bytes 3145732
  89.9 30.2 %all-to-all-start.1 = ((f32[16,128,128]{1,2,0:T(8,128)}), f32[16,128,128]{1,2,0:T(8,128)}, u32[]{:S(2)}, u32[]{:S(2)}) async-start(f32[16,128,128]{1,2,0:T(8,128)} %bitcast.8), calls=%async_computation.1 | async-start | bytes 2097152 | tf_op jit(solution)/shard_map/all_to_all | solution.py:37
  94.2 235.6 %reduce-scatter.5.cloned.1.call-start = ((), (), s32[]{:S(2)}) async-start(), calls=%async_computation.10 | async-start | bytes 7077888
  99.8 3.1 copy-start.6
  128.5 4.2 copy-start.1
  139.2 12.1 %slice-start = ((s8[6291456]{0:T(1024)(128)(4,1)}), s8[2097152]{0:T(1024)(128)(4,1)S(1)}, s32[]{:S(2)}) async-start(s8[6291456]{0:T(1024)(128)(4,1)} %bitcast.215), calls=%async_computation.11 | async-start | bytes 4194304
  143.4 4.8 %copy-start = (f32[64,64,64]{2,0,1:T(8,128)S(1)}, f32[64,64,64]{2,0,1:T(8,128)}, u32[]{:S(2)}) copy-start(f32[64,64,64]{2,0,1:T(8,128)} %copy.271) | copy-start | bytes 3145732
  143.4 7.9 %slice-start.1 = ((s8[6291456]{0:T(1024)(128)(4,1)}), s8[4194304]{0:T(1024)(128)(4,1)S(1)}, s32[]{:S(2)}) async-start(s8[6291456]{0:T(1024)(128)(4,1)} %bitcast.215), calls=%async_computation.12 | async-start | bytes 8388608
  151.3 2.4 copy-start.17
  153.7 3.8 copy-start.7
  173.9 1.3 copy-start.4
  187.6 5.6 %copy-start.2 = (f32[64,64,64]{2,1,0:T(8,128)S(1)}, f32[64,64,64]{2,1,0:T(8,128)}, u32[]{:S(2)}) copy-start(f32[64,64,64]{2,1,0:T(8,128)} %copy-done.1) | copy-start | bytes 3145732
  193.3 2.9 copy-start.14
  193.3 2.9 copy-start.18
  196.2 1.6 copy-start.15
  196.2 2.2 copy-start.16
  207.8 4.3 copy-start.5
  227.7 48.1 %all-to-all-start.2 = ((f32[8,256,128]{1,2,0:T(8,128)}), f32[8,256,128]{1,2,0:T(8,128)}, u32[]{:S(2)}, u32[]{:S(2)}) async-start(f32[8,256,128]{1,2,0:T(8,128)} %bitcast.24), calls=%async_computation.2 | async-start | bytes 2097152 | tf_op jit(solution)/shard_map/all_to_all | solution.py:37
  232.0 3.5 copy-start.3
  275.8 38.3 %all-to-all-start.4 = ((f32[16,128,128]{1,2,0:T(8,128)}), f32[16,128,128]{1,2,0:T(8,128)S(1)}, u32[]{:S(2)}, u32[]{:S(2)}) async-start(f32[16,128,128]{1,2,0:T(8,128)} %bitcast.41), calls=%async_computation.4 | async-start | bytes 2097152 | tf_op jit(solution)/shard_map/all_to_all | solution.py:37
  279.4 139.7 %all-reduce.3.cloned.1.call-start = ((), (), s32[]{:S(2)}) async-start(), calls=%async_computation.8 | async-start | bytes 1146880 | tf_op jit(solution)/shard_map/psum | solution.py:179
  314.1 1.0 copy-start.13
  316.1 4.6 copy-start.9
  325.6 1.0 copy-start.10
  326.6 1.4 copy-start.11
  327.5 127.4 %all-reduce.5.cloned.1.call-start = ((), (), s32[]{:S(2)}) async-start(), calls=%async_computation.9 | async-start | bytes 1572864 | tf_op jit(solution)/shard_map/psum | solution.py:150
  333.1 90.7 %all-to-all-start.5 = ((f32[2,256,512]{1,2,0:T(8,128)}), f32[2,256,512]{1,2,0:T(8,128)S(1)}, u32[]{:S(2)}, u32[]{:S(2)}) async-start(f32[2,256,512]{1,2,0:T(8,128)} %add_bitcast_fusion), calls=%async_computation.5 | async-start | bytes 2097152 | tf_op jit(solution)/shard_map/all_to_all | solution.py:37
Sparse Core Ops, SparseCore 0:
  11.0 92.0 all-gather.1
  207.9 94.5 reduce-scatter.4
  327.6 91.5 all-reduce.2
  421.3 33.5 all-reduce.4

commit v2 on v1

--- a/solution.py
+++ b/solution.py
@@ -69,26 +69,37 @@
     total = length * row_count
     tokens = length // block_count
 
-    stacked = jnp.concatenate(
-        [
-            jnp.concatenate([gate_right, value_right], axis=2)[:, None],
-            jnp.concatenate([gate_left, value_left], axis=2)[:, None],
-            jnp.concatenate([output_right, output_left], axis=2)[:, None],
-        ],
-        axis=1,
-    )
-    factors = lax.all_gather(stacked, "block", axis=0, tiled=True)
-    right_pair = factors[:, 0]
-    gate_l, value_l = factors[:, 1, :, :breadth], factors[:, 1, :, breadth:]
-    out_r, out_l = factors[:, 2, :, :breadth], factors[:, 2, :, breadth:]
-    right_all = lax.all_gather(seq_right, ROWS, axis=0, tiled=True)
-    left_turned = lax.all_gather(seq_left.transpose(1, 2, 0), ROWS, axis=2, tiled=True)
-
-    def to_channels(values):
-        arrived = trade(values.reshape(row_count, mine, length), ROWS)
-        return arrived.transpose(1, 0, 2).reshape(mine, total)
-
-    own = to_channels(source)
+    def whole(former, latter):
+        return lax.all_gather(jnp.concatenate([former, latter], axis=2), "block", axis=0, tiled=True)
+
+    right_pair = whole(gate_right, value_right)
+    left_pair = whole(gate_left, value_left)
+    output_pair = whole(output_right, output_left)
+    gate_l, value_l = left_pair[:, :, :breadth], left_pair[:, :, breadth:]
+    out_r, out_l = output_pair[:, :, :breadth], output_pair[:, :, breadth:]
+
+    def copies(values):
+        return jnp.broadcast_to(values[None], (row_count, *values.shape))
+
+    right_rows = copies(seq_right.transpose(1, 0, 2).reshape(seq_block, length))
+    left_rows = copies(seq_left.transpose(1, 2, 0).reshape(-1, length))
+    arrived = trade(
+        jnp.concatenate([source.reshape(row_count, mine, length), right_rows, left_rows], axis=1), ROWS
+    )
+    own = arrived[:, :mine].transpose(1, 0, 2).reshape(mine, total)
+    right_all = (
+        arrived[:, mine : mine + seq_block]
+        .reshape(row_count, seq_block, seq_right.shape[0], seq_block)
+        .transpose(0, 2, 1, 3)
+        .reshape(seq_count, seq_block, seq_block)
+    )
+    left_turned = (
+        arrived[:, mine + seq_block :]
+        .reshape(row_count, seq_count, seq_count, seq_left.shape[0])
+        .transpose(1, 2, 0, 3)
+        .reshape(seq_count, seq_count, seq_block)
+    )
+
     own_blocks = own.reshape(mine, seq_count, seq_block)
     sectioned_seq = contract("cai,aij->caj", own_blocks, right_all)
     seq_mixed = jnp.sum(left_turned[None] * sectioned_seq[:, :, None, :], axis=1)
@@ -104,9 +115,9 @@
             .reshape(blocks, breadth, tokens)
         )
 
-    across = upstream.reshape(channels, block_count, tokens).transpose(1, 0, 2)
+    mixed, late = lax.optimization_barrier((to_tokens(mixed_own), upstream))
+    across = late.reshape(channels, block_count, tokens).transpose(1, 0, 2)
     up = unpack(trade(pack(across), "block"), tokens).reshape(blocks, breadth, tokens)
-    mixed = to_tokens(mixed_own)
 
     pair = contract("bit,bij->bjt", mixed, right_pair)
     gate_s, value_s = pair[:, :breadth], pair[:, breadth:]
@@ -116,20 +127,27 @@
     output_s = contract("bit,bij->bjt", hidden, out_r)
     layer = mixed + contract("bjt,jbk->kjt", output_s, out_l)
 
-    def to_home(values):
-        pieces = values.reshape(block_count, channels, tokens)
-        arrived = unpack(trade(pack(pieces), "block"), tokens)
-        return arrived.transpose(1, 0, 2).reshape(channels, length)
-
-    layer_out = to_home(layer)
+    leaving, up = lax.optimization_barrier(
+        (pack(layer.reshape(block_count, channels, tokens)), up)
+    )
+    layer_out = unpack(trade(leaving, "block"), tokens).transpose(1, 0, 2).reshape(channels, length)
+
+    grad_scale = 1.0 / math.sqrt(total)
+
+    def summed(former, latter):
+        both = jnp.concatenate([former, latter], axis=2) * grad_scale
+        part = lax.psum_scatter(both, "block", scatter_dimension=0, tiled=True)
+        return part
 
     grad_out_l = contract("bjt,kjt->jbk", output_s, up)
     output_back = contract("jbk,kjt->bjt", out_l, up)
     grad_out_r = contract("bit,bjt->bij", hidden, output_back)
+    output_grads = summed(grad_out_r, grad_out_l)
     hidden_back = contract("bij,bjt->bit", out_r, output_back)
     gate_back, value_back = pullback(hidden_back)
     grad_gate_l = contract("bjt,kjt->jbk", gate_s, gate_back)
     grad_value_l = contract("bjt,kjt->jbk", value_s, value_back)
+    left_grads = summed(grad_gate_l, grad_value_l)
     pair_back = jnp.concatenate(
         [contract("jbk,kjt->bjt", gate_l, gate_back), contract("jbk,kjt->bjt", value_l, value_back)],
         axis=1,
@@ -137,17 +155,7 @@
     grad_right_pair = contract("bit,bjt->bij", mixed, pair_back)
     mixed_back = up + contract("bij,bjt->bit", right_pair, pair_back)
 
-    grad_scale = 1.0 / math.sqrt(total)
-    grads = jnp.concatenate(
-        [
-            grad_right_pair[:, None],
-            jnp.concatenate([grad_gate_l, grad_value_l], axis=2)[:, None],
-            jnp.concatenate([grad_out_r, grad_out_l], axis=2)[:, None],
-        ],
-        axis=1,
-    )
-    grads = lax.psum_scatter(grads * grad_scale, "block", scatter_dimension=0, tiled=True)
-    grads = lax.psum(grads, ROWS)
+    right_grads = summed(grad_right_pair[:, :, :breadth], grad_right_pair[:, :, breadth:])
 
     pieces = (
         mixed_back.reshape(block_count, row_count, mine, tokens)
@@ -168,29 +176,38 @@
     gain_row = lax.dynamic_update_slice_in_dim(
         jnp.zeros((width,), jnp.float32), gain_part, block_index * channels + row_index * mine, 0
     )
+    right_size = seq_right.size // LANES
+    left_size = seq_left.size // LANES
     tail = jnp.concatenate(
         [
-            right_part.reshape(-1, LANES),
-            left_part.reshape(-1, LANES),
-            gain_row.reshape(-1, LANES),
+            right_part.reshape(row_count, right_size, LANES),
+            left_part.reshape(seq_count, seq_count, row_count, seq_left.shape[0])
+            .transpose(2, 0, 1, 3)
+            .reshape(row_count, left_size, LANES),
+            copies(gain_row.reshape(-1, LANES)),
         ],
-        axis=0,
-    )
-    tail = lax.psum(tail * grad_scale, EVERY)
-    right_rows = right_part.size // LANES
-    left_rows = left_part.size // LANES
-    right_sum = lax.dynamic_slice_in_dim(
-        tail[:right_rows].reshape(right_part.shape), row_index * seq_right.shape[0], seq_right.shape[0]
-    )
-    left_sum = lax.dynamic_slice_in_dim(
-        tail[right_rows : right_rows + left_rows].reshape(left_part.shape),
-        row_index * seq_left.shape[0],
-        seq_left.shape[0],
-        axis=2,
-    ).transpose(2, 0, 1)
+        axis=1,
+    )
+    tail_rows = tail.shape[1]
+    spare = -tail_rows % block_count
+    tail = jnp.pad(tail, ((0, 0), (0, spare), (0, 0)))
+    tail = trade(tail.reshape(everyone, -1, LANES), EVERY)
+    tail = jnp.sum(tail, axis=0) * grad_scale
+    tail = trade(jnp.broadcast_to(tail[None], (block_count, *tail.shape)), "block").reshape(-1, LANES)
+    right_sum = tail[:right_size].reshape(seq_right.shape)
+    left_sum = (
+        tail[right_size : right_size + left_size]
+        .reshape(seq_count, seq_count, seq_left.shape[0])
+        .transpose(2, 0, 1)
+    )
     gain_sum = lax.dynamic_slice_in_dim(
-        tail[right_rows + left_rows :].reshape(-1), block_index * channels, channels
-    )
+        tail[right_size + left_size : tail_rows].reshape(-1), block_index * channels, channels
+    )
+    grads = jnp.stack([right_grads, left_grads, output_grads], axis=1)
+    if row_count == 2:
+        grads = grads + lax.ppermute(grads, ROWS, [(0, 1), (1, 0)])
+    else:
+        grads = lax.psum(grads, ROWS)
     return (
         layer_out.reshape(inputs.shape),
         grad_inputs.reshape(inputs.shape),

time: 470 us -> 387 us (0.82)
  waiting for transfers between devices: 230 us -> 135 us
  blocking collectives: 18.1 us -> 0 us
  starting transfers between devices: 25.5 us -> 39.6 us
  other arithmetic: 21.7 us -> 31.8 us
    psum x2 -> x0, waiting for transfers between devices: 111 us -> none  [the longest x1 82.5 us: body(): tail = lax.psum(tail * grad_scale, EVERY)]
    all_gather x2 -> x0, blocking collectives: 18.1 us -> none  [the longest x1 9.39 us: body(): lax.all_gather(seq_left.transpose(1, 2, 0), ROWS, axis=2, tiled=True)]
    all_to_all x6 -> x8, waiting for transfers between devices: 119 us -> 135 us  [trade(): return lax.all_to_all(rows, axes, split_axis=0, concat_axis=0, tiled=True)]
    another operation x2, local copies, waits for them, and re-layouts: 2.45 us -> 16.2 us  [pack(): pieces.reshape(parts, fold, channels // fold, tokens).transpose(0, 2, 1, 3)]
    all_to_all x6 -> x8, starting transfers between devices: 25.2 us -> 36.6 us  [trade(): return lax.all_to_all(rows, axes, split_axis=0, concat_axis=0, tiled=True)]
    unnamed x59 -> x68, local copies, waits for them, and re-layouts: 20 us -> 8.92 us
    another operation x3 -> x0, local copies, waits for them, and re-layouts: 8.94 us -> none  [body(): unpack(trade(pack(across), 'block'), tokens)]
    optimization_barrier x0 -> x2, local copies, waits for them, and re-layouts: none -> 7.45 us  [body(): mixed, late = lax.optimization_barrier((to_tokens(mixed_own), upstream))]
  transfers between devices with their start and end apart: 10 -> 15, of which waited for: 7 -> 7; matrix products, arithmetic and copies ran while one was open for 19% -> 42% of each run, Pallas kernels for 0% -> 0%
where the time goes in v2:
time: 387 us; the launch traced here: 383 us
  waiting for transfers between devices  135 us (35%)
  local copies, waits for them, and re-layouts  94.4 us (24%)
  matrix products  66.7 us (17%)
  starting transfers between devices  39.6 us (10%)
  other arithmetic  31.8 us (8%)
  between operations  15 us (4%)
    all_to_all x8, waiting for transfers between devices, trade(): return lax.all_to_all(rows, axes, split_axis=0, concat_axis=0, tiled=True)  135 us
    dot_general x18, matrix products, contract(): jnp.einsum(pattern, former, latter, precision=lax.Precision.HIGH, preferr...  66.7 us
    all_to_all x8, starting transfers between devices, trade(): return lax.all_to_all(rows, axes, split_axis=0, concat_axis=0, tiled=True)  36.6 us
    another operation x2, local copies, waits for them, and re-layouts, pack(): pieces.reshape(parts, fold, channels // fold, tokens).transpose(0, 2, 1, 3)  16.2 us
    unnamed x68, local copies, waits for them, and re-layouts  8.92 us
    slice x3, local copies, waits for them, and re-layouts, body(): gate_s, value_s = (pair[:, :breadth], pair[:, breadth:])  8.69 us
  transfers between devices with their start and end apart: 15, of which 7 were waited for; matrix products, arithmetic and copies ran while one was open for 42% of the time, Pallas kernels for 0%

profile of v2, /device:TPU:0, one launch (start us, length us, event | category | flops | bytes accessed | tf_op | source)
XLA Modules:
  0.0 382.8 jit_solution(5334618367177116851)
XLA Ops:
  7.2 2.0 pad_maximum_fusion.7
  9.3 1.9 pad_maximum_fusion.6
  13.1 4.3 %all-to-all-start = ((f32[2,392,512]{2,1,0:T(8,128)}), f32[2,392,512]{2,1,0:T(8,128)S(1)}, u32[]{:S(2)}, u32[]{:S(2)}) async-start(f32[2,392,512]{2,1,0:T(8,128)} %pad_maximum_fusion.1), calls=%async_computation | async-start | bytes 3211264 | tf_op jit(solution)/shard_map/all_to_all | solution.py:37
  18.4 19.5 %all-to-all-done = f32[2,392,512]{2,1,0:T(8,128)S(1)} async-done(((f32[2,392,512]{2,1,0:T(8,128)}), f32[2,392,512]{2,1,0:T(8,128)S(1)}, u32[]{:S(2)}, u32[]{:S(2)}) %all-to-all-start) | async-done | bytes 1605664 | tf_op jit(solution)/shard_map/all_to_all | solution.py:37
  42.3 1.6 copy.273
  44.2 2.1 multiply_reduce_fusion.2
  49.2 5.2 %all-to-all-start.1 = ((f32[16,128,128]{1,2,0:T(8,128)}), f32[16,128,128]{1,2,0:T(8,128)S(1)}, u32[]{:S(2)}, u32[]{:S(2)}) async-start(f32[16,128,128]{1,2,0:T(8,128)} %bitcast.191), calls=%async_computation.1 | async-start | bytes 2097152 | tf_op jit(solution)/shard_map/all_to_all | solution.py:37
  54.4 3.6 copy.278
  58.0 34.8 %all-to-all-done.1 = f32[16,128,128]{1,2,0:T(8,128)S(1)} async-done(((f32[16,128,128]{1,2,0:T(8,128)}), f32[16,128,128]{1,2,0:T(8,128)S(1)}, u32[]{:S(2)}, u32[]{:S(2)}) %all-to-all-start.1) | async-done | bytes 1048608 | tf_op jit(solution)/shard_map/all_to_all | solution.py:37
  93.7 1.8 reshape_reshape.26
  95.5 2.0 copy.277
  97.5 2.4 reshape.153
  99.9 2.5 copy.313
  102.5 4.9 %copy.288 = f32[64,64,64]{2,0,1:T(8,128)} copy(f32[64,64,64]{1,0,2:T(8,128)} %reshape.153) | data formatting | bytes 2097152 | tf_op jit(solution)/shard_map/optimization_barrier | solution.py:118
  107.4 2.4 copy.369
  109.8 4.2 %all-to-all-start.2 = ((f32[8,256,128]{1,2,0:T(8,128)}), f32[8,256,128]{1,2,0:T(8,128)}, u32[]{:S(2)}, u32[]{:S(2)}) async-start(f32[8,256,128]{1,2,0:T(8,128)} %bitcast.187), calls=%async_computation.2 | async-start | bytes 2097152 | tf_op jit(solution)/shard_map/all_to_all | solution.py:37
  114.4 3.4 fusion.56
  117.8 2.1 fusion.54
  119.9 3.8 copy.283
  123.7 2.8 copy.285
  126.5 4.2 %fusion.12 = f32[64,64,64]{2,1,0:T(8,128)S(1)} fusion(f32[64,64,64]{2,0,1:T(8,128)} %copy.283, f32[64,64,128]{2,1,0:T(8,128)} %all-gather.6.cloned.1.call-done), kind=kOutput, calls=%fused_computation.25 | convolution fusion | flops 100663296 | bytes 4194304 | tf_op jit(solution)/shard_map/bjt,jbk->kjt/dot_general | solution.py:14
  130.7 4.7 %bitcast_multiply_fusion.1 = (f32[64,64,64]{2,0,1:T(8,128)}, f32[64,64,64]{2,1,0:T(8,128)}) fusion(f32[64,64,64]{2,1,0:T(8,128)S(1)} %fusion.12, f32[64,64,64]{2,0,1:T(8,128)S(1)} %copy-done.12, f32[64,64,128]{2,1,0:T(8,128)S(1)} %copy-done), kind=kOutput, calls=%fused_computation.16 | convolution fusion | flops 103022592 | bytes 6291456 | tf_op jit(solution)/shard_map/bjt,jbk->kjt/dot_general | solution.py:14
  135.4 5.2 %fusion.16 = f32[64,64,64]{2,1,0:T(8,128)S(1)} fusion(f32[64,64,128]{2,1,0:T(8,128)} %all-gather.4.cloned.1.call-done, f32[64,64,64]{2,0,1:T(8,128)} %get-tuple-element.90), kind=kOutput, calls=%fused_computation.29 | convolution fusion | flops 100663296 | bytes 4194304 | tf_op jit(solution)/shard_map/bit,bij->bjt/dot_general | solution.py:14
  142.0 4.6 %bitcast_add_fusion = f32[64,64,64]{2,0,1:T(8,128)} fusion(f32[64,64,64]{2,0,1:T(8,128)S(1)} %copy-done.19, f32[64,64,64]{2,1,0:T(8,128)S(1)} %fusion.16, f32[64,64,128]{2,1,0:T(8,128)S(1)} %copy-done.2), kind=kOutput, calls=%fused_computation.14 | convolution fusion | flops 100925440 | bytes 5242880 | tf_op jit(solution)/shard_map/bjt,jbk->kjt/dot_general | solution.py:14
  146.6 4.1 %copy.289 = f32[64,64,64]{1,0,2:T(8,128)} copy(f32[64,64,64]{2,0,1:T(8,128)} %bitcast_add_fusion) | data formatting | bytes 2097152 | tf_op jit(solution)/shard_map/add | solution.py:128
  150.7 13.4 %reshape_reshape.27 = f32[8,2,256,64]{2,1,0,3:T(2,128)} reshape(f32[64,64,64]{1,0,2:T(8,128)} %copy.289) | data formatting | bytes 2097152 | tf_op jit(solution)/shard_map/reshape;reshape | solution.py:26
  164.1 2.8 copy.290
  166.9 3.2 copy.292
  170.1 6.9 %fusion.32 = f32[64,64,64]{0,2,1:T(8,128)} fusion(f32[64,64,128]{2,1,0:T(8,128)} %all-gather.4.cloned.1.call-done, f32[64,64,64]{2,1,0:T(8,128)} %bitcast.170), kind=kOutput, calls=%fused_computation.46 | convolution fusion | flops 100663296 | bytes 4194304 | tf_op jit(solution)/shard_map/jbk,kjt->bjt/dot_general | solution.py:14
  176.9 3.8 copy.297
  180.8 3.4 fusion.18
  184.2 3.1 fusion.53
  187.3 2.0 fusion.5
  189.3 1.8 fusion.57
  191.1 1.9 maximum_multiply_fusion
  193.5 4.2 %fusion.41 = f32[64,64,64]{0,2,1:T(8,128)S(1)} fusion(f32[64,64,64]{2,0,1:T(8,128)} %copy-done.11, f32[64,64,128]{2,1,0:T(8,128)} %all-gather.6.cloned.1.call-done), kind=kOutput, calls=%fused_computation.47 | convolution fusion | flops 100663296 | bytes 4194304 | tf_op jit(solution)/shard_map/jbk,kjt->bjt/dot_general | solution.py:14
  197.7 3.5 fusion.44
  201.2 2.5 pad_maximum_fusion
  203.7 5.5 %copy.304 = f32[64,128,64]{1,2,0:T(8,128)} copy(f32[64,128,64]{0,2,1:T(8,128)} %pad_maximum_fusion) | data formatting | bytes 4194304 | tf_op jit(solution)/shard_map/concatenate | solution.py:151
  209.2 4.1 %convolution_multiply_fusion = f32[64,64,128]{2,1,0:T(8,128)} fusion(f32[64,64,64]{2,1,0:T(8,128)S(1)} %copy-done.7, f32[64,128,64]{1,2,0:T(8,128)} %copy.304), kind=kOutput, calls=%fused_computation.49 | convolution fusion | flops 201850880 | bytes 5242880 | tf_op jit(solution)/shard_map/bit,bjt->bij/dot_general | solution.py:14
  214.9 5.4 %convolution_add_fusion = f32[64,64,64]{2,1,0:T(8,128)} fusion(f32[64,64,64]{2,1,0:T(8,128)S(1)} %bitcast.171, f32[64,64,128]{2,1,0:T(8,128)} %all-gather.8.cloned.1.call-done, f32[64,128,64]{1,2,0:T(8,128)} %copy.304), kind=kOutput, calls=%fused_computation.50 | convolution fusion | flops 201588736 | bytes 6291456 | tf_op jit(solution)/shard_map/bij,bjt->bit/dot_general | solution.py:14
  220.3 3.2 copy.305
  223.5 2.7 reshape_reshape.30
  226.2 2.3 copy.306
  228.5 5.9 %all-to-all-start.4 = ((f32[16,128,128]{1,2,0:T(8,128)}), f32[16,128,128]{1,2,0:T(8,128)}, u32[]{:S(2)}, u32[]{:S(2)}) async-start(f32[16,128,128]{1,2,0:T(8,128)} %bitcast.188), calls=%async_computation.4 | async-start | bytes 2097152 | tf_op jit(solution)/shard_map/all_to_all | solution.py:37
  234.7 5.3 %fusion.29 = f32[64,64,64]{2,1,0:T(8,128)S(1)} fusion(f32[64,64,64]{2,1,0:T(8,128)} %copy.297, f32[64,64,64]{2,0,1:T(8,128)} %get-tuple-element.90), kind=kOutput, calls=%fused_computation.43 | convolution fusion | flops 100663296 | bytes 3145728 | tf_op jit(solution)/shard_map/bit,bjt->bij/dot_general | solution.py:14
  240.0 4.1 %fusion.25 = f32[64,64,64]{2,1,0:T(8,128)S(1)} fusion(f32[64,64,64]{2,1,0:T(8,128)S(1)} %bitcast.172, f32[64,64,64]{2,1,0:T(8,128)S(1)} %copy-done.10), kind=kOutput, calls=%fused_computation.38 | convolution fusion | flops 100663296 | bytes 3145728 | tf_op jit(solution)/shard_map/bjt,kjt->jbk/dot_general | solution.py:14
  244.1 2.0 maximum_multiply_fusion.1
  246.0 25.3 %all-to-all-done.4 = f32[16,128,128]{1,2,0:T(8,128)} async-done(((f32[16,128,128]{1,2,0:T(8,128)}), f32[16,128,128]{1,2,0:T(8,128)}, u32[]{:S(2)}, u32[]{:S(2)}) %all-to-all-start.4) | async-done | bytes 1048608 | tf_op jit(solution)/shard_map/all_to_all | solution.py:37
  271.4 5.5 %all-to-all-start.3 = ((f32[8,256,128]{1,2,0:T(8,128)}), f32[8,256,128]{1,2,0:T(8,128)}, u32[]{:S(2)}, u32[]{:S(2)}) async-start(f32[8,256,128]{1,2,0:T(8,128)} %bitcast.21), calls=%async_computation.3 | async-start | bytes 2097152 | tf_op jit(solution)/shard_map/all_to_all | solution.py:37
  279.2 2.6 copy.308
  281.8 5.8 %multiply_reduce_fusion = (f32[8,8,128]{2,1,0:T(8,128)S(1)}, f32[256,8,128]{2,1,0:T(8,128)}) fusion(f32[256,8,128]{2,1,0:T(8,128)} %copy.308, f32[256,8,128]{2,1,0:T(8,128)S(1)} %copy-done.15, f32[8,8,128]{2,1,0:T(8,128)S(1)} %mul.143), kind=kLoop, calls=%fused_computation | loop fusion | flops 8118272 | bytes 3211264 | tf_op jit(solution)/shard_map/reduce_sum | solution.py:168
  287.8 1.8 fusion.47
  291.6 21.2 %all-to-all-done.3 = f32[8,256,128]{1,2,0:T(8,128)} async-done(((f32[8,256,128]{1,2,0:T(8,128)}), f32[8,256,128]{1,2,0:T(8,128)}, u32[]{:S(2)}, u32[]{:S(2)}) %all-to-all-start.3) | async-done | bytes 1048608 | tf_op jit(solution)/shard_map/all_to_all | solution.py:37
  312.8 3.8 all-to-all-start.6
  318.4 18.9 %all-to-all-done.6 = f32[16,72,128]{2,1,0:T(8,128)S(1)} async-done(((f32[16,72,128]{2,1,0:T(8,128)}), f32[16,72,128]{2,1,0:T(8,128)S(1)}, u32[]{:S(2)}, u32[]{:S(2)}) %all-to-all-start.6) | async-done | bytes 589856 | tf_op jit(solution)/shard_map/all_to_all | solution.py:37
  337.4 3.6 all-to-all-start.5
  341.1 2.1 pad_maximum_fusion.2
  343.2 2.0 collective-permute-start
  345.2 10.7 %all-to-all-done.5 = f32[2,256,512]{1,2,0:T(8,128)S(1)} async-done(((f32[2,256,512]{1,2,0:T(8,128)}), f32[2,256,512]{1,2,0:T(8,128)S(1)}, u32[]{:S(2)}, u32[]{:S(2)}) %all-to-all-start.5) | async-done | bytes 1048608 | tf_op jit(solution)/shard_map/all_to_all | solution.py:37
  356.6 4.0 %all-to-all-start.7 = ((f32[8,72,128]{2,1,0:T(8,128)}), f32[8,72,128]{2,1,0:T(8,128)S(1)}, u32[]{:S(2)}, u32[]{:S(2)}) async-start(f32[8,72,128]{2,1,0:T(8,128)} %broadcast_in_dim.41), calls=%async_computation.7 | async-start | bytes 589824 | tf_op jit(solution)/shard_map/all_to_all | solution.py:37
  362.0 1.9 copy.321
  364.3 2.2 reshape_reshape.31
  366.5 4.6 %all-to-all-done.7 = f32[8,72,128]{2,1,0:T(8,128)S(1)} async-done(((f32[8,72,128]{2,1,0:T(8,128)}), f32[8,72,128]{2,1,0:T(8,128)S(1)}, u32[]{:S(2)}, u32[]{:S(2)}) %all-to-all-start.7) | async-done | bytes 294944 | tf_op jit(solution)/shard_map/all_to_all | solution.py:37
  (129 shorter events, 28.7 us)
Async XLA Ops:
  7.2 4.0 %copy-start.23 = (f32[512,1,512]{2,1,0:T(1,128)S(1)}, f32[512,1,512]{2,1,0:T(1,128)}, u32[]{:S(2)}) copy-start(f32[512,1,512]{2,1,0:T(1,128)} %param.11) | copy-start | bytes 3145732
  7.2 4.1 %copy-start.29 = (f32[4,128,128]{2,1,0:T(8,128)S(1)}, f32[4,128,128]{2,1,0:T(8,128)}, u32[]{:S(2)}) copy-start(f32[4,128,128]{2,1,0:T(8,128)} %param.13) | copy-start | bytes 786436
  7.2 107.2 %all-gather.8.cloned.1.call-start = ((), (), s32[]{:S(2)}) async-start(), calls=%async_computation.13 | async-start | bytes 2359296 | tf_op jit(solution)/shard_map/all_gather | solution.py:73
  9.2 2.3 copy-start.30
  9.2 117.2 %all-gather.6.cloned.1.call-start = ((), (), s32[]{:S(2)}) async-start(), calls=%async_computation.12 | async-start | bytes 2359296 | tf_op jit(solution)/shard_map/all_gather | solution.py:73
  13.1 4.3 %copy-start.27 = (f32[8,64,64]{2,1,0:T(8,128)S(1)}, f32[8,64,64]{2,1,0:T(8,128)}, u32[]{:S(2)}) copy-start(f32[8,64,64]{2,1,0:T(8,128)} %param.21) | copy-start | bytes 393220
  13.1 4.3 %copy-start.28 = (f32[8,64,64]{2,1,0:T(8,128)S(1)}, f32[8,64,64]{2,1,0:T(8,128)}, u32[]{:S(2)}) copy-start(f32[8,64,64]{2,1,0:T(8,128)} %param.20) | copy-start | bytes 393220
  13.1 5.2 %copy-start.31 = (f32[512]{0:T(512)S(1)}, f32[512]{0:T(512)}, u32[]{:S(2)}) copy-start(f32[512]{0:T(512)} %param.15) | copy-start | bytes 6148
  13.1 24.8 %all-to-all-start = ((f32[2,392,512]{2,1,0:T(8,128)}), f32[2,392,512]{2,1,0:T(8,128)S(1)}, u32[]{:S(2)}, u32[]{:S(2)}) async-start(f32[2,392,512]{2,1,0:T(8,128)} %pad_maximum_fusion.1), calls=%async_computation | async-start | bytes 3211264 | tf_op jit(solution)/shard_map/all_to_all | solution.py:37
  17.4 118.0 %all-gather.4.cloned.1.call-start = ((), (), s32[]{:S(2)}) async-start(), calls=%async_computation.11 | async-start | bytes 2359296 | tf_op jit(solution)/shard_map/all_gather | solution.py:73
  37.9 2.7 copy-start.20
  40.7 3.3 copy-start.21
  40.7 3.3 slice-start
  44.0 3.9 %copy-start.14 = (f32[256,8,128]{2,1,0:T(8,128)}, f32[256,8,128]{2,1,0:T(8,128)S(1)}, u32[]{:S(2)}) copy-start(f32[256,8,128]{2,1,0:T(8,128)S(1)} %copy.273) | copy-start | bytes 3145732
  47.9 1.3 copy-start.17
  49.2 43.7 %all-to-all-start.1 = ((f32[16,128,128]{1,2,0:T(8,128)}), f32[16,128,128]{1,2,0:T(8,128)S(1)}, u32[]{:S(2)}, u32[]{:S(2)}) async-start(f32[16,128,128]{1,2,0:T(8,128)} %bitcast.191), calls=%async_computation.1 | async-start | bytes 2097152 | tf_op jit(solution)/shard_map/all_to_all | solution.py:37
  102.5 11.9 %copy-start.6 = (f32[64,64,64]{2,1,0:T(8,128)}, f32[64,64,64]{2,1,0:T(8,128)S(1)}, u32[]{:S(2)}) copy-start(f32[64,64,64]{2,1,0:T(8,128)S(1)} %copy.313) | copy-start | bytes 3145732
  109.8 57.1 %all-to-all-start.2 = ((f32[8,256,128]{1,2,0:T(8,128)}), f32[8,256,128]{1,2,0:T(8,128)}, u32[]{:S(2)}, u32[]{:S(2)}) async-start(f32[8,256,128]{1,2,0:T(8,128)} %bitcast.187), calls=%async_computation.2 | async-start | bytes 2097152 | tf_op jit(solution)/shard_map/all_to_all | solution.py:37
  114.0 227.0 %reduce-scatter.6.cloned.1.call-start = ((), (), s32[]{:S(2)}) async-start(), calls=%async_computation.15 | async-start | bytes 2359296 | tf_op jit(solution)/shard_map/reduce_scatter | solution.py:139
  126.5 4.2 %copy-start = (f32[64,64,128]{2,1,0:T(8,128)S(1)}, f32[64,64,128]{2,1,0:T(8,128)}, u32[]{:S(2)}) copy-start(f32[64,64,128]{2,1,0:T(8,128)} %all-gather.6.cloned.1.call-done) | copy-start | bytes 6291460
  126.5 4.2 %copy-start.12 = (f32[64,64,64]{2,0,1:T(8,128)S(1)}, f32[64,64,64]{2,0,1:T(8,128)}, u32[]{:S(2)}) copy-start(f32[64,64,64]{2,0,1:T(8,128)} %copy.285) | copy-start | bytes 3145732
  135.4 6.6 %copy-start.2 = (f32[64,64,128]{2,1,0:T(8,128)S(1)}, f32[64,64,128]{2,1,0:T(8,128)}, u32[]{:S(2)}) copy-start(f32[64,64,128]{2,1,0:T(8,128)} %all-gather.4.cloned.1.call-done) | copy-start | bytes 6291460
  135.4 6.6 %copy-start.19 = (f32[64,64,64]{2,0,1:T(8,128)S(1)}, f32[64,64,64]{2,0,1:T(8,128)}, u32[]{:S(2)}) copy-start(f32[64,64,64]{2,0,1:T(8,128)} %copy.288) | copy-start | bytes 3145732
  140.6 1.4 copy-start.9
  180.7 3.4 copy-start.13
  184.2 3.1 copy-start.4
  184.2 3.1 copy-start.18
  187.3 2.0 copy-start.8
  189.3 1.8 copy-start.11
  193.1 148.0 %reduce-scatter.4.cloned.1.call-start = ((), (), s32[]{:S(2)}) async-start(), calls=%async_computation.14 | async-start | bytes 2359296 | tf_op jit(solution)/shard_map/reduce_scatter | solution.py:139
  193.5 4.2 %copy-start.1 = (f32[64,64,128]{2,1,0:T(8,128)S(1)}, f32[64,64,128]{2,1,0:T(8,128)}, u32[]{:S(2)}) copy-start(f32[64,64,128]{2,1,0:T(8,128)} %all-gather.6.cloned.1.call-done) | copy-start | bytes 6291460
  193.5 4.2 %copy-start.5 = (f32[64,64,64]{2,1,0:T(8,128)S(1)}, f32[64,64,64]{2,1,0:T(8,128)}, u32[]{:S(2)}) copy-start(f32[64,64,64]{2,1,0:T(8,128)} %copy-done.4) | copy-start | bytes 3145732
  203.7 5.5 %copy-start.7 = (f32[64,64,64]{2,1,0:T(8,128)S(1)}, f32[64,64,64]{2,1,0:T(8,128)}, u32[]{:S(2)}) copy-start(f32[64,64,64]{2,1,0:T(8,128)} %copy-done.6) | copy-start | bytes 3145732
  213.3 1.6 copy-start.3
  228.5 42.8 %all-to-all-start.4 = ((f32[16,128,128]{1,2,0:T(8,128)}), f32[16,128,128]{1,2,0:T(8,128)}, u32[]{:S(2)}, u32[]{:S(2)}) async-start(f32[16,128,128]{1,2,0:T(8,128)} %bitcast.188), calls=%async_computation.4 | async-start | bytes 2097152 | tf_op jit(solution)/shard_map/all_to_all | solution.py:37
  234.4 106.6 %reduce-scatter.8.cloned.1.call-start = ((), (), s32[]{:S(2)}) async-start(), calls=%async_computation.16 | async-start | bytes 2359296 | tf_op jit(solution)/shard_map/reduce_scatter | solution.py:139
  234.7 5.3 %copy-start.10 = (f32[64,64,64]{2,1,0:T(8,128)S(1)}, f32[64,64,64]{2,1,0:T(8,128)}, u32[]{:S(2)}) copy-start(f32[64,64,64]{2,1,0:T(8,128)} %copy-done.9) | copy-start | bytes 3145732
  271.4 41.4 %all-to-all-start.3 = ((f32[8,256,128]{1,2,0:T(8,128)}), f32[8,256,128]{1,2,0:T(8,128)}, u32[]{:S(2)}, u32[]{:S(2)}) async-start(f32[8,256,128]{1,2,0:T(8,128)} %bitcast.21), calls=%async_computation.3 | async-start | bytes 2097152 | tf_op jit(solution)/shard_map/all_to_all | solution.py:37
  278.1 3.7 copy-start.15
  287.6 2.3 copy-start.16
  290.7 25.9 %copy-start.22 = (f32[2,512,128]{2,1,0:T(8,128)S(1)}, f32[2,512,128]{2,1,0:T(8,128)}, u32[]{:S(2)}) copy-start(f32[2,512,128]{2,1,0:T(8,128)} %copy-done.21) | copy-start | bytes 1572868
  312.8 24.6 %all-to-all-start.6 = ((f32[16,72,128]{2,1,0:T(8,128)}), f32[16,72,128]{2,1,0:T(8,128)S(1)}, u32[]{:S(2)}, u32[]{:S(2)}) async-start(f32[16,72,128]{2,1,0:T(8,128)} %bitcast.195), calls=%async_computation.6 | async-start | bytes 1179648 | tf_op jit(solution)/shard_map/all_to_all | solution.py:37
  337.4 18.6 %all-to-all-start.5 = ((f32[2,256,512]{1,2,0:T(8,128)}), f32[2,256,512]{1,2,0:T(8,128)S(1)}, u32[]{:S(2)}, u32[]{:S(2)}) async-start(f32[2,256,512]{1,2,0:T(8,128)} %add_bitcast_fusion), calls=%async_computation.5 | async-start | bytes 2097152 | tf_op jit(solution)/shard_map/all_to_all | solution.py:37
  343.2 30.0 %collective-permute-start = (f32[8,3,64,128]{3,2,0,1:T(8,128)}, f32[8,3,64,128]{3,2,0,1:T(8,128)}, u32[]{:S(2)}, u32[]{:S(2)}) collective-permute-start(f32[8,3,64,128]{3,2,0,1:T(8,128)} %pad_maximum_fusion.2), channel_id=1, source_target_pairs={{0,1},{1,0},{2,3},{3,2},{4,5},{5,4},{6,7},{7,6},{8,9},{9,8},{10,11... | collective-permute-start | bytes 2359304 | tf_op jit(solution)/shard_map/ppermute | solution.py:208
  356.6 14.5 %all-to-all-start.7 = ((f32[8,72,128]{2,1,0:T(8,128)}), f32[8,72,128]{2,1,0:T(8,128)S(1)}, u32[]{:S(2)}, u32[]{:S(2)}) async-start(f32[8,72,128]{2,1,0:T(8,128)} %broadcast_in_dim.41), calls=%async_computation.7 | async-start | bytes 589824 | tf_op jit(solution)/shard_map/all_to_all | solution.py:37
  364.0 9.2 %copy-start.24 = (f32[8,64,128]{2,1,0:T(8,128)S(1)}, f32[8,64,128]{2,1,0:T(8,128)}, u32[]{:S(2)}) copy-start(f32[8,64,128]{2,1,0:T(8,128)} %reduce-scatter.6.cloned.1.call-done) | copy-start | bytes 786436
  364.0 9.2 %copy-start.25 = (f32[8,64,128]{2,1,0:T(8,128)S(1)}, f32[8,64,128]{2,1,0:T(8,128)}, u32[]{:S(2)}) copy-start(f32[8,64,128]{2,1,0:T(8,128)} %reduce-scatter.4.cloned.1.call-done) | copy-start | bytes 786436
  364.0 9.2 %copy-start.26 = (f32[8,64,128]{2,1,0:T(8,128)S(1)}, f32[8,64,128]{2,1,0:T(8,128)}, u32[]{:S(2)}) copy-start(f32[8,64,128]{2,1,0:T(8,128)} %reduce-scatter.8.cloned.1.call-done) | copy-start | bytes 786436
Sparse Core Ops, SparseCore 0:
  10.2 31.8 all-gather.7
  44.3 46.9 all-gather.5
  93.4 30.9 all-gather.3
  193.2 36.9 reduce-scatter.5
  232.4 48.0 reduce-scatter.3
  282.6 48.5 reduce-scatter.7

commit v3 on v2

--- a/solution.py
+++ b/solution.py
@@ -35,6 +35,17 @@
 
 def trade(rows, axes):
     return lax.all_to_all(rows, axes, split_axis=0, concat_axis=0, tiled=True)
+
+
+def trade_rows(rows):
+    if rows.shape[0] != 2:
+        return trade(rows, ROWS)
+    me = lax.axis_index("dp") * lax.axis_size("seq") + lax.axis_index("seq")
+    kept = lax.dynamic_index_in_dim(rows, me, keepdims=False)
+    sent = lax.dynamic_index_in_dim(rows, 1 - me, keepdims=False)
+    got = lax.ppermute(sent, ROWS, [(0, 1), (1, 0)])
+    first = me == 0
+    return jnp.stack([jnp.where(first, kept, got), jnp.where(first, got, kept)])
 
 
 def body(
@@ -73,18 +84,14 @@
         return lax.all_gather(jnp.concatenate([former, latter], axis=2), "block", axis=0, tiled=True)
 
     right_pair = whole(gate_right, value_right)
-    left_pair = whole(gate_left, value_left)
-    output_pair = whole(output_right, output_left)
-    gate_l, value_l = left_pair[:, :, :breadth], left_pair[:, :, breadth:]
-    out_r, out_l = output_pair[:, :, :breadth], output_pair[:, :, breadth:]
 
     def copies(values):
         return jnp.broadcast_to(values[None], (row_count, *values.shape))
 
     right_rows = copies(seq_right.transpose(1, 0, 2).reshape(seq_block, length))
     left_rows = copies(seq_left.transpose(1, 2, 0).reshape(-1, length))
-    arrived = trade(
-        jnp.concatenate([source.reshape(row_count, mine, length), right_rows, left_rows], axis=1), ROWS
+    arrived = trade_rows(
+        jnp.concatenate([source.reshape(row_count, mine, length), right_rows, left_rows], axis=1)
     )
     own = arrived[:, :mine].transpose(1, 0, 2).reshape(mine, total)
     right_all = (
@@ -106,18 +113,23 @@
     gain = lax.dynamic_slice_in_dim(seq_gain, row_index * mine, mine)
     mixed_own = own + gain[:, None] * seq_mixed.reshape(mine, total)
 
-    def to_tokens(values):
-        pieces = values.reshape(mine, everyone, tokens).transpose(1, 0, 2)
-        arrived = unpack(trade(pack(pieces), EVERY), tokens)
-        return (
-            arrived.reshape(row_count, block_count, mine, tokens)
-            .transpose(1, 0, 2, 3)
-            .reshape(blocks, breadth, tokens)
-        )
-
-    mixed, late = lax.optimization_barrier((to_tokens(mixed_own), upstream))
-    across = late.reshape(channels, block_count, tokens).transpose(1, 0, 2)
-    up = unpack(trade(pack(across), "block"), tokens).reshape(blocks, breadth, tokens)
+    leaving = pack(mixed_own.reshape(mine, everyone, tokens).transpose(1, 0, 2))
+    across = pack(upstream.reshape(channels, block_count, tokens).transpose(1, 0, 2))
+    leaving, across = lax.optimization_barrier((leaving, across))
+    tokens_in, across, gate_left, value_left, output_right, output_left = lax.optimization_barrier(
+        (trade(leaving, EVERY), across, gate_left, value_left, output_right, output_left)
+    )
+    left_pair = whole(gate_left, value_left)
+    output_pair = whole(output_right, output_left)
+    gate_l, value_l = left_pair[:, :, :breadth], left_pair[:, :, breadth:]
+    out_r, out_l = output_pair[:, :, :breadth], output_pair[:, :, breadth:]
+    mixed = (
+        unpack(tokens_in, tokens)
+        .reshape(row_count, block_count, mine, tokens)
+        .transpose(1, 0, 2, 3)
+        .reshape(blocks, breadth, tokens)
+    )
+    up = unpack(trade(across, "block"), tokens).reshape(blocks, breadth, tokens)
 
     pair = contract("bit,bij->bjt", mixed, right_pair)
     gate_s, value_s = pair[:, :breadth], pair[:, breadth:]
@@ -130,14 +142,16 @@
     leaving, up = lax.optimization_barrier(
         (pack(layer.reshape(block_count, channels, tokens)), up)
     )
-    layer_out = unpack(trade(leaving, "block"), tokens).transpose(1, 0, 2).reshape(channels, length)
+    layer_home = trade(leaving, "block")
 
     grad_scale = 1.0 / math.sqrt(total)
 
     def summed(former, latter):
         both = jnp.concatenate([former, latter], axis=2) * grad_scale
         part = lax.psum_scatter(both, "block", scatter_dimension=0, tiled=True)
-        return part
+        if row_count == 2:
+            return part + lax.ppermute(part, ROWS, [(0, 1), (1, 0)])
+        return lax.psum(part, ROWS)
 
     grad_out_l = contract("bjt,kjt->jbk", output_s, up)
     output_back = contract("jbk,kjt->bjt", out_l, up)
@@ -162,15 +176,17 @@
         .transpose(1, 0, 2, 3)
         .reshape(everyone, mine, tokens)
     )
-    back_own = unpack(trade(pack(pieces), EVERY), tokens).transpose(1, 0, 2).reshape(mine, total)
+    returning, layer_home = lax.optimization_barrier((pack(pieces), layer_home))
+    back_own = unpack(trade(returning, EVERY), tokens).transpose(1, 0, 2).reshape(mine, total)
+    layer_out = unpack(layer_home, tokens).transpose(1, 0, 2).reshape(channels, length)
     gain_part = jnp.sum(back_own * seq_mixed.reshape(mine, total), axis=1)
     seq_back = (gain[:, None] * back_own).reshape(mine, seq_count, seq_block)
     left_part = jnp.sum(sectioned_seq[:, :, None, :] * seq_back[:, None, :, :], axis=0)
     sectioned_back = jnp.sum(left_turned[None] * seq_back[:, None, :, :], axis=2)
     right_part = contract("cai,caj->aij", own_blocks, sectioned_back)
     grad_own = back_own + contract("aij,caj->cai", right_all, sectioned_back).reshape(mine, total)
-    grad_inputs = trade(
-        grad_own.reshape(mine, row_count, length).transpose(1, 0, 2), ROWS
+    grad_inputs = trade_rows(
+        grad_own.reshape(mine, row_count, length).transpose(1, 0, 2)
     ).reshape(channels, length)
 
     gain_row = lax.dynamic_update_slice_in_dim(
@@ -203,23 +219,18 @@
     gain_sum = lax.dynamic_slice_in_dim(
         tail[right_size + left_size : tail_rows].reshape(-1), block_index * channels, channels
     )
-    grads = jnp.stack([right_grads, left_grads, output_grads], axis=1)
-    if row_count == 2:
-        grads = grads + lax.ppermute(grads, ROWS, [(0, 1), (1, 0)])
-    else:
-        grads = lax.psum(grads, ROWS)
     return (
         layer_out.reshape(inputs.shape),
         grad_inputs.reshape(inputs.shape),
         right_sum,
         left_sum,
         gain_sum,
-        grads[:, 0, :, :breadth],
-        grads[:, 1, :, :breadth],
-        grads[:, 0, :, breadth:],
-        grads[:, 1, :, breadth:],
-        grads[:, 2, :, :breadth],
-        grads[:, 2, :, breadth:],
+        right_grads[:, :, :breadth],
+        left_grads[:, :, :breadth],
+        right_grads[:, :, breadth:],
+        left_grads[:, :, breadth:],
+        output_grads[:, :, :breadth],
+        output_grads[:, :, breadth:],
     )
 
 

time: 387 us -> 386 us (level)
  blocking collectives: 0 us -> 31.4 us
  waiting for transfers between devices: 135 us -> 119 us
  local copies, waits for them, and re-layouts: 94.4 us -> 84.3 us
  starting transfers between devices: 39.6 us -> 33.5 us
    all_to_all x8 -> x5, waiting for transfers between devices: 135 us -> 65.2 us  [trade(): return lax.all_to_all(rows, axes, split_axis=0, concat_axis=0, tiled=True)]
    all_to_all x0 -> x1, blocking collectives: none -> 31.4 us  [trade(): return lax.all_to_all(rows, axes, split_axis=0, concat_axis=0, tiled=True)]
    reduce_scatter x3, waiting for transfers between devices: 0.06 us -> 23 us  [summed(): part = lax.psum_scatter(both, 'block', scatter_dimension=0, tiled=True)]
    all_gather x3, waiting for transfers between devices: 0.02 us -> 17.1 us  [whole(): lax.all_gather(jnp.concatenate([former, latter], axis=2), 'block', axis=0...]
    ppermute x1 -> x5, waiting for transfers between devices: 0.01 us -> 13.8 us  [the longest x2 13.8 us: trade_rows(): got = lax.ppermute(sent, ROWS, [(0, 1), (1, 0)])]
    all_to_all x8 -> x5, starting transfers between devices: 36.6 us -> 24.3 us  [trade(): return lax.all_to_all(rows, axes, split_axis=0, concat_axis=0, tiled=True)]
    another operation x2, local copies, waits for them, and re-layouts: 16.2 us -> 4.81 us  [pack(): pieces.reshape(parts, fold, channels // fold, tokens).transpose(0, 2, 1, 3)]
    optimization_barrier x2 -> x0, local copies, waits for them, and re-layouts: 7.45 us -> none  [body(): mixed, late = lax.optimization_barrier((to_tokens(mixed_own), upstream))]
  transfers between devices with their start and end apart: 15 -> 16, of which waited for: 7 -> 7; matrix products, arithmetic and copies ran while one was open for 42% -> 34% of each run, Pallas kernels for 0% -> 0%
where the time goes in v3:
time: 386 us; the launch traced here: 380 us
  waiting for transfers between devices  119 us (31%)
  local copies, waits for them, and re-layouts  84.3 us (22%)
  matrix products  67.5 us (17%)
  starting transfers between devices  33.5 us (9%)
  blocking collectives  31.4 us (8%)
  other arithmetic  29.2 us (8%)
  between operations  15.1 us (4%)
    dot_general x18, matrix products, contract(): jnp.einsum(pattern, former, latter, precision=lax.Precision.HIGH, preferr...  67.5 us
    all_to_all x5, waiting for transfers between devices, trade(): return lax.all_to_all(rows, axes, split_axis=0, concat_axis=0, tiled=True)  65.2 us
    all_to_all x1, blocking collectives, trade(): return lax.all_to_all(rows, axes, split_axis=0, concat_axis=0, tiled=True)  31.4 us
    all_to_all x5, starting transfers between devices, trade(): return lax.all_to_all(rows, axes, split_axis=0, concat_axis=0, tiled=True)  24.3 us
    reduce_scatter x3, waiting for transfers between devices, summed(): part = lax.psum_scatter(both, 'block', scatter_dimension=0, tiled=True)  23 us
    all_gather x3, waiting for transfers between devices, whole(): lax.all_gather(jnp.concatenate([former, latter], axis=2), 'block', axis=0...  17.1 us
    ppermute x2, waiting for transfers between devices, trade_rows(): got = lax.ppermute(sent, ROWS, [(0, 1), (1, 0)])  13.8 us
    unnamed x75, local copies, waits for them, and re-layouts  11.1 us
  transfers between devices with their start and end apart: 16, of which 7 were waited for; matrix products, arithmetic and copies ran while one was open for 34% of the time, Pallas kernels for 0%

profile of v3, /device:TPU:0, one launch (start us, length us, event | category | flops | bytes accessed | tf_op | source)
XLA Modules:
  0.0 380.2 jit_solution(6753241916516201891)
XLA Ops:
  10.1 2.9 collective-permute-start
  14.0 2.3 copy.229
  17.5 13.8 %collective-permute-done = f32[392,512]{1,0:T(8,128)} collective-permute-done((f32[392,512]{1,0:T(8,128)}, f32[392,512]{1,0:T(8,128)}, u32[]{:S(2)}, u32[]{:S(2)}) %collective-permute-start) | collective-permute-done | bytes 802848 | tf_op jit(solution)/shard_map/ppermute | solution.py:46
  33.6 1.6 copy.221
  36.1 1.6 convolution_bitcast_fusion
  37.7 2.5 copy.226
  40.5 2.4 multiply_reduce_fusion.2
  44.6 1.7 reshape.148
  46.5 31.4 %all_to_all.30 = f32[16,128,128]{1,2,0:T(8,128)S(1)} all-to-all(f32[16,128,128]{1,2,0:T(8,128)S(1)} %bitcast.197), channel_id=1, replica_groups=mesh['groups'=2,'block'=8,'dp'=1,'seq'=2] {'dp','seq','block'}, dimensions={0} | all-to-all | bytes 2097152 | tf_op jit(solution)/shard_map/all_to_all | solution.py:37
  79.8 4.3 %all-to-all-start.1 = ((f32[8,256,128]{1,2,0:T(8,128)}), f32[8,256,128]{1,2,0:T(8,128)}, u32[]{:S(2)}, u32[]{:S(2)}) async-start(f32[8,256,128]{1,2,0:T(8,128)} %bitcast.20), calls=%async_computation.1 | async-start | bytes 2097152 | tf_op jit(solution)/shard_map/all_to_all | solution.py:37
  85.4 1.8 reshape_reshape.30
  87.2 2.0 copy.232
  89.3 2.4 reshape.153
  91.7 2.4 copy.267
  94.1 5.0 %copy.242 = f32[64,64,64]{2,0,1:T(8,128)} copy(f32[64,64,64]{1,0,2:T(8,128)} %reshape.153) | data formatting | bytes 2097152 | tf_op jit(solution)/shard_map/reshape | solution.py:130
  99.0 3.4 fusion.68
  102.4 2.1 fusion.64
  104.5 3.8 %copy.237 = f32[64,64,64]{2,0,1:T(8,128)} copy(f32[64,64,64]{1,2,0:T(8,128)} %get-tuple-element.83) | data formatting | bytes 2097152 | tf_op jit(solution)/shard_map/slice | solution.py:135
  108.3 2.9 copy.239
  111.2 16.3 %all-to-all-done.1 = f32[8,256,128]{1,2,0:T(8,128)} async-done(((f32[8,256,128]{1,2,0:T(8,128)}), f32[8,256,128]{1,2,0:T(8,128)}, u32[]{:S(2)}, u32[]{:S(2)}) %all-to-all-start.1) | async-done | bytes 1048608 | tf_op jit(solution)/shard_map/all_to_all | solution.py:37
  127.5 3.3 copy.245
  130.8 4.2 %fusion.12 = f32[64,64,64]{2,1,0:T(8,128)S(1)} fusion(f32[64,64,64]{2,0,1:T(8,128)} %copy.237, f32[64,64,128]{2,1,0:T(8,128)} %all-gather.6.cloned.1.call-done), kind=kOutput, calls=%fused_computation.35 | convolution fusion | flops 100663296 | bytes 4194304 | tf_op jit(solution)/shard_map/bjt,jbk->kjt/dot_general | solution.py:14
  135.0 4.6 %bitcast_multiply_fusion.1 = (f32[64,64,64]{2,0,1:T(8,128)}, f32[64,64,64]{2,1,0:T(8,128)}) fusion(f32[64,64,64]{2,1,0:T(8,128)S(1)} %fusion.12, f32[64,64,64]{2,0,1:T(8,128)S(1)} %copy-done.13, f32[64,64,128]{2,1,0:T(8,128)S(1)} %copy-done), kind=kOutput, calls=%fused_computation.26 | convolution fusion | flops 103022592 | bytes 6291456 | tf_op jit(solution)/shard_map/bjt,jbk->kjt/dot_general | solution.py:14
  139.6 17.1 %all-gather.4.cloned.1.call-done = f32[64,64,128]{2,1,0:T(8,128)} async-done(((f32[8,64,128]{2,1,0:T(8,128)}), f32[64,64,128]{2,1,0:T(8,128)}) %all-gather.4.cloned.1.call-update) | async-done | bytes 2097168 | tf_op jit(solution)/shard_map/all_gather | solution.py:84
  156.7 5.2 %fusion.16 = f32[64,64,64]{2,1,0:T(8,128)S(1)} fusion(f32[64,64,128]{2,1,0:T(8,128)} %all-gather.4.cloned.1.call-done, f32[64,64,64]{2,0,1:T(8,128)} %get-tuple-element.100), kind=kOutput, calls=%fused_computation.39 | convolution fusion | flops 100663296 | bytes 4194304 | tf_op jit(solution)/shard_map/bit,bij->bjt/dot_general | solution.py:14
  163.2 4.6 %bitcast_add_fusion = f32[64,64,64]{2,0,1:T(8,128)} fusion(f32[64,64,64]{2,0,1:T(8,128)S(1)} %copy-done.20, f32[64,64,64]{2,1,0:T(8,128)S(1)} %fusion.16, f32[64,64,128]{2,1,0:T(8,128)S(1)} %copy-done.2), kind=kOutput, calls=%fused_computation.24 | convolution fusion | flops 100925440 | bytes 5242880 | tf_op jit(solution)/shard_map/bjt,jbk->kjt/dot_general | solution.py:14
  167.8 4.2 %copy.243 = f32[64,64,64]{1,0,2:T(8,128)} copy(f32[64,64,64]{2,0,1:T(8,128)} %bitcast_add_fusion) | data formatting | bytes 2097152 | tf_op jit(solution)/shard_map/add | solution.py:140
  172.0 3.3 reshape_reshape.31
  175.4 2.9 copy.244
  178.3 7.1 %fusion.25 = f32[64,64,64]{2,1,0:T(8,128)} fusion(f32[64,64,64]{2,1,0:T(8,128)S(1)} %bitcast.175, f32[64,64,64]{2,1,0:T(8,128)} %copy-done.12), kind=kOutput, calls=%fused_computation.48 | convolution fusion | flops 100663296 | bytes 3145728 | tf_op jit(solution)/shard_map/bjt,kjt->jbk/dot_general | solution.py:14
  185.5 4.7 %fusion.32 = f32[64,64,64]{0,2,1:T(8,128)} fusion(f32[64,64,128]{2,1,0:T(8,128)S(1)} %copy-done.3, f32[64,64,64]{2,1,0:T(8,128)S(1)} %bitcast.176), kind=kOutput, calls=%fused_computation.56 | convolution fusion | flops 100663296 | bytes 4194304 | tf_op jit(solution)/shard_map/jbk,kjt->bjt/dot_general | solution.py:14
  190.1 4.2 %copy.249 = f32[64,64,64]{2,1,0:T(8,128)} copy(f32[64,64,64]{0,2,1:T(8,128)} %fusion.32) | data formatting | bytes 2097152 | tf_op jit(solution)/shard_map/jbk,kjt->bjt/transpose | solution.py:14
  194.4 5.2 %fusion.29 = f32[64,64,64]{2,1,0:T(8,128)S(1)} fusion(f32[64,64,64]{2,1,0:T(8,128)} %copy.249, f32[64,64,64]{2,0,1:T(8,128)} %get-tuple-element.100), kind=kOutput, calls=%fused_computation.53 | convolution fusion | flops 100663296 | bytes 3145728 | tf_op jit(solution)/shard_map/bit,bjt->bij/dot_general | solution.py:14
  199.6 1.9 maximum_multiply_fusion.1
  201.6 3.4 fusion.18
  205.0 2.0 fusion.5
  207.5 1.8 fusion.69
  209.8 3.1 fusion.63
  212.9 1.9 maximum_multiply_fusion
  214.8 4.4 %all-to-all-start.2 = ((f32[8,256,128]{1,2,0:T(8,128)}), f32[8,256,128]{1,2,0:T(8,128)}, u32[]{:S(2)}, u32[]{:S(2)}) async-start(f32[8,256,128]{1,2,0:T(8,128)} %bitcast.192), calls=%async_computation.2 | async-start | bytes 2097152 | tf_op jit(solution)/shard_map/all_to_all | solution.py:37
  219.3 4.2 %fusion.41 = f32[64,64,64]{0,2,1:T(8,128)S(1)} fusion(f32[64,64,64]{2,0,1:T(8,128)} %copy-done.11, f32[64,64,128]{2,1,0:T(8,128)} %all-gather.6.cloned.1.call-done), kind=kOutput, calls=%fused_computation.57 | convolution fusion | flops 100663296 | bytes 4194304 | tf_op jit(solution)/shard_map/jbk,kjt->bjt/dot_general | solution.py:14
  223.6 3.5 fusion.44
  227.0 2.5 pad_maximum_fusion
  229.6 5.5 %copy.256 = f32[64,128,64]{1,2,0:T(8,128)} copy(f32[64,128,64]{0,2,1:T(8,128)} %pad_maximum_fusion) | data formatting | bytes 4194304 | tf_op jit(solution)/shard_map/concatenate | solution.py:165
  235.0 5.4 %convolution_add_fusion = f32[64,64,64]{2,1,0:T(8,128)} fusion(f32[64,64,64]{2,1,0:T(8,128)S(1)} %bitcast.177, f32[64,64,128]{2,1,0:T(8,128)} %all-gather.8.cloned.1.call-done, f32[64,128,64]{1,2,0:T(8,128)} %copy.256), kind=kOutput, calls=%fused_computation.60 | convolution fusion | flops 201588736 | bytes 6291456 | tf_op jit(solution)/shard_map/bij,bjt->bit/dot_general | solution.py:14
  240.5 2.2 copy.257
  242.7 1.5 reshape_reshape.33
  244.2 2.5 copy.258
  246.6 7.7 %all-to-all-done.2 = f32[8,256,128]{1,2,0:T(8,128)} async-done(((f32[8,256,128]{1,2,0:T(8,128)}), f32[8,256,128]{1,2,0:T(8,128)}, u32[]{:S(2)}, u32[]{:S(2)}) %all-to-all-start.2) | async-done | bytes 1048608 | tf_op jit(solution)/shard_map/all_to_all | solution.py:37
  254.3 4.5 %all-to-all-start.3 = ((f32[16,128,128]{1,2,0:T(8,128)}), f32[16,128,128]{1,2,0:T(8,128)}, u32[]{:S(2)}, u32[]{:S(2)}) async-start(f32[16,128,128]{1,2,0:T(8,128)} %bitcast.193), calls=%async_computation.3 | async-start | bytes 2097152 | tf_op jit(solution)/shard_map/all_to_all | solution.py:37
  259.1 4.1 %convolution_multiply_fusion = f32[64,64,128]{2,1,0:T(8,128)} fusion(f32[64,64,64]{2,1,0:T(8,128)S(1)} %copy-done.9, f32[64,128,64]{1,2,0:T(8,128)} %copy.256), kind=kOutput, calls=%fused_computation.59 | convolution fusion | flops 201850880 | bytes 5242880 | tf_op jit(solution)/shard_map/bit,bjt->bij/dot_general | solution.py:14
  263.2 34.4 %all-to-all-done.3 = f32[16,128,128]{1,2,0:T(8,128)} async-done(((f32[16,128,128]{1,2,0:T(8,128)}), f32[16,128,128]{1,2,0:T(8,128)}, u32[]{:S(2)}, u32[]{:S(2)}) %all-to-all-start.3) | async-done | bytes 1048608 | tf_op jit(solution)/shard_map/all_to_all | solution.py:37
  300.0 2.5 copy.261
  302.5 5.8 %multiply_reduce_fusion = (f32[8,8,128]{2,1,0:T(8,128)S(1)}, f32[256,8,128]{2,1,0:T(8,128)}) fusion(f32[256,8,128]{2,1,0:T(8,128)} %copy.261, f32[256,8,128]{2,1,0:T(8,128)S(1)} %copy-done.15, f32[8,8,128]{2,1,0:T(8,128)S(1)} %mul.145), kind=kLoop, calls=%fused_computation | loop fusion | flops 8118272 | bytes 3211264 | tf_op jit(solution)/shard_map/reduce_sum | solution.py:184
  308.5 1.8 fusion.49
  312.3 5.7 %all-to-all-start.4 = ((f32[16,72,128]{2,1,0:T(8,128)}), f32[16,72,128]{2,1,0:T(8,128)S(1)}, u32[]{:S(2)}, u32[]{:S(2)}) async-start(f32[16,72,128]{2,1,0:T(8,128)} %bitcast.202), calls=%async_computation.4 | async-start | bytes 1179648 | tf_op jit(solution)/shard_map/all_to_all | solution.py:37
  319.2 2.0 collective-permute-start.1
  321.2 1.4 copy.291
  322.6 1.9 copy.275
  324.9 1.9 collective-permute-start.3
  326.8 22.9 %reduce-scatter.4.cloned.1.call-done = f32[8,64,128]{2,1,0:T(8,128)} async-done(((f32[64,64,128]{2,1,0:T(8,128)}), f32[8,64,128]{2,1,0:T(8,128)}) %reduce-scatter.4.cloned.1.call-update) | async-done | bytes 262160 | tf_op jit(solution)/shard_map/reduce_scatter | solution.py:151
  351.2 2.0 copy.276
  355.1 5.5 %all-to-all-start.5 = ((f32[8,72,128]{2,1,0:T(8,128)}), f32[8,72,128]{2,1,0:T(8,128)S(1)}, u32[]{:S(2)}, u32[]{:S(2)}) async-start(f32[8,72,128]{2,1,0:T(8,128)} %broadcast_in_dim.41), calls=%async_computation.5 | async-start | bytes 589824 | tf_op jit(solution)/shard_map/all_to_all | solution.py:37
  364.2 6.8 %all-to-all-done.5 = f32[8,72,128]{2,1,0:T(8,128)S(1)} async-done(((f32[8,72,128]{2,1,0:T(8,128)}), f32[8,72,128]{2,1,0:T(8,128)S(1)}, u32[]{:S(2)}, u32[]{:S(2)}) %all-to-all-start.5) | async-done | bytes 294944 | tf_op jit(solution)/shard_map/all_to_all | solution.py:37
  (148 shorter events, 31.1 us)
Async XLA Ops:
  7.2 1.4 copy-start.32
  7.2 1.7 copy-start.33
  7.2 91.8 %all-gather.8.cloned.1.call-start = ((), (), s32[]{:S(2)}) async-start(), calls=%async_computation.11 | async-start | bytes 2359296 | tf_op jit(solution)/shard_map/all_gather | solution.py:84
  9.0 4.0 %copy-start.23 = (f32[8,64,64]{2,1,0:T(8,128)S(1)}, f32[8,64,64]{2,1,0:T(8,128)}, u32[]{:S(2)}) copy-start(f32[8,64,64]{2,1,0:T(8,128)} %param.18) | copy-start | bytes 393220
  9.0 4.0 %copy-start.24 = (f32[8,64,64]{2,1,0:T(8,128)S(1)}, f32[8,64,64]{2,1,0:T(8,128)}, u32[]{:S(2)}) copy-start(f32[8,64,64]{2,1,0:T(8,128)} %param.16) | copy-start | bytes 393220
  10.1 21.1 %collective-permute-start = (f32[392,512]{1,0:T(8,128)}, f32[392,512]{1,0:T(8,128)}, u32[]{:S(2)}, u32[]{:S(2)}) collective-permute-start(f32[392,512]{1,0:T(8,128)} %dynamic-slice_bitcast_fusion), channel_id=1, source_target_pairs={{0,1},{1,0},{2,3},{3,2},{4,5},{5,4},{6,7},{7,6},{8,9},{9,8},{10,11... | collective-permute-start | bytes 2408456 | tf_op jit(solution)/shard_map/ppermute | solution.py:46
  13.9 116.8 %all-gather.6.cloned.1.call-start = ((), (), s32[]{:S(2)}) async-start(), calls=%async_computation.10 | async-start | bytes 2359296 | tf_op jit(solution)/shard_map/all_gather | solution.py:84
  14.0 3.5 copy-start.34
  35.3 0.8 copy-start.21
  43.3 3.1 copy-start.17
  46.3 31.6 %copy-start.25 = (f32[8,64,64]{2,1,0:T(8,128)S(1)}, f32[8,64,64]{2,1,0:T(8,128)}, u32[]{:S(2)}) copy-start(f32[8,64,64]{2,1,0:T(8,128)} %param.19) | copy-start | bytes 393220
  46.4 31.6 %copy-start.26 = (f32[8,64,64]{2,1,0:T(8,128)S(1)}, f32[8,64,64]{2,1,0:T(8,128)}, u32[]{:S(2)}) copy-start(f32[8,64,64]{2,1,0:T(8,128)} %param.17) | copy-start | bytes 393220
  46.5 32.4 %copy-start.27 = (f32[8,64,64]{2,1,0:T(8,128)S(1)}, f32[8,64,64]{2,1,0:T(8,128)}, u32[]{:S(2)}) copy-start(f32[8,64,64]{2,1,0:T(8,128)} %param.21) | copy-start | bytes 393220
  46.5 32.4 %copy-start.28 = (f32[8,64,64]{2,1,0:T(8,128)S(1)}, f32[8,64,64]{2,1,0:T(8,128)}, u32[]{:S(2)}) copy-start(f32[8,64,64]{2,1,0:T(8,128)} %param.20) | copy-start | bytes 393220
  78.8 77.8 %all-gather.4.cloned.1.call-start = ((), (), s32[]{:S(2)}) async-start(), calls=%async_computation.9 | async-start | bytes 2359296 | tf_op jit(solution)/shard_map/all_gather | solution.py:84
  79.8 47.7 %all-to-all-start.1 = ((f32[8,256,128]{1,2,0:T(8,128)}), f32[8,256,128]{1,2,0:T(8,128)}, u32[]{:S(2)}, u32[]{:S(2)}) async-start(f32[8,256,128]{1,2,0:T(8,128)} %bitcast.20), calls=%async_computation.1 | async-start | bytes 2097152 | tf_op jit(solution)/shard_map/all_to_all | solution.py:37
  84.0 240.7 %reduce-scatter.8.cloned.1.call-start = ((), (), s32[]{:S(2)}) async-start(), calls=%async_computation.14 | async-start | bytes 2359296 | tf_op jit(solution)/shard_map/reduce_scatter | solution.py:151
  94.1 5.0 %copy-start.8 = (f32[64,64,64]{2,1,0:T(8,128)}, f32[64,64,64]{2,1,0:T(8,128)S(1)}, u32[]{:S(2)}) copy-start(f32[64,64,64]{2,1,0:T(8,128)S(1)} %copy.267) | copy-start | bytes 3145732
  130.8 4.2 %copy-start = (f32[64,64,128]{2,1,0:T(8,128)S(1)}, f32[64,64,128]{2,1,0:T(8,128)}, u32[]{:S(2)}) copy-start(f32[64,64,128]{2,1,0:T(8,128)} %all-gather.6.cloned.1.call-done) | copy-start | bytes 6291460
  130.8 4.2 %copy-start.13 = (f32[64,64,64]{2,0,1:T(8,128)S(1)}, f32[64,64,64]{2,0,1:T(8,128)}, u32[]{:S(2)}) copy-start(f32[64,64,64]{2,0,1:T(8,128)} %copy.239) | copy-start | bytes 3145732
  156.7 6.5 %copy-start.2 = (f32[64,64,128]{2,1,0:T(8,128)S(1)}, f32[64,64,128]{2,1,0:T(8,128)}, u32[]{:S(2)}) copy-start(f32[64,64,128]{2,1,0:T(8,128)} %all-gather.4.cloned.1.call-done) | copy-start | bytes 6291460
  156.7 6.5 %copy-start.20 = (f32[64,64,64]{2,0,1:T(8,128)S(1)}, f32[64,64,64]{2,0,1:T(8,128)}, u32[]{:S(2)}) copy-start(f32[64,64,64]{2,0,1:T(8,128)} %copy.242) | copy-start | bytes 3145732
  161.8 1.4 copy-start.12
  175.4 2.9 copy-start.4
  178.3 7.1 %copy-start.3 = (f32[64,64,128]{2,1,0:T(8,128)S(1)}, f32[64,64,128]{2,1,0:T(8,128)}, u32[]{:S(2)}) copy-start(f32[64,64,128]{2,1,0:T(8,128)} %all-gather.4.cloned.1.call-done) | copy-start | bytes 6291460
  194.4 5.2 %copy-start.18 = (f32[64,64,64]{2,1,0:T(8,128)S(1)}, f32[64,64,64]{2,1,0:T(8,128)}, u32[]{:S(2)}) copy-start(f32[64,64,64]{2,1,0:T(8,128)} %fusion.25) | copy-start | bytes 3145732
  201.5 123.4 %reduce-scatter.6.cloned.1.call-start = ((), (), s32[]{:S(2)}) async-start(), calls=%async_computation.13 | async-start | bytes 2359296 | tf_op jit(solution)/shard_map/reduce_scatter | solution.py:151
  201.6 3.5 copy-start.19
  205.0 4.3 %copy-start.6 = (f32[64,64,64]{2,1,0:T(8,128)}, f32[64,64,64]{2,1,0:T(8,128)S(1)}, u32[]{:S(2)}) copy-start(f32[64,64,64]{2,1,0:T(8,128)S(1)} %fusion.18) | copy-start | bytes 3145732
  205.0 2.5 copy-start.10
  207.5 1.8 copy-start.11
  207.5 2.3 copy-start.14
  214.8 39.5 %all-to-all-start.2 = ((f32[8,256,128]{1,2,0:T(8,128)}), f32[8,256,128]{1,2,0:T(8,128)}, u32[]{:S(2)}, u32[]{:S(2)}) async-start(f32[8,256,128]{1,2,0:T(8,128)} %bitcast.192), calls=%async_computation.2 | async-start | bytes 2097152 | tf_op jit(solution)/shard_map/all_to_all | solution.py:37
  219.3 4.3 %copy-start.1 = (f32[64,64,128]{2,1,0:T(8,128)S(1)}, f32[64,64,128]{2,1,0:T(8,128)}, u32[]{:S(2)}) copy-start(f32[64,64,128]{2,1,0:T(8,128)} %all-gather.6.cloned.1.call-done) | copy-start | bytes 6291460
  219.3 4.3 %copy-start.7 = (f32[64,64,64]{2,1,0:T(8,128)S(1)}, f32[64,64,64]{2,1,0:T(8,128)}, u32[]{:S(2)}) copy-start(f32[64,64,64]{2,1,0:T(8,128)} %copy-done.6) | copy-start | bytes 3145732
  229.6 5.5 %copy-start.5 = (f32[8,2,256,64]{3,2,1,0:T(8,128)S(1)}, f32[8,2,256,64]{3,2,1,0:T(8,128)}, u32[]{:S(2)}) copy-start(f32[8,2,256,64]{3,2,1,0:T(8,128)} %copy.245) | copy-start | bytes 3145732
  244.2 14.9 %copy-start.9 = (f32[64,64,64]{2,1,0:T(8,128)S(1)}, f32[64,64,64]{2,1,0:T(8,128)}, u32[]{:S(2)}) copy-start(f32[64,64,64]{2,1,0:T(8,128)} %copy-done.8) | copy-start | bytes 3145732
  254.3 43.2 %all-to-all-start.3 = ((f32[16,128,128]{1,2,0:T(8,128)}), f32[16,128,128]{1,2,0:T(8,128)}, u32[]{:S(2)}, u32[]{:S(2)}) async-start(f32[16,128,128]{1,2,0:T(8,128)} %bitcast.193), calls=%async_computation.3 | async-start | bytes 2097152 | tf_op jit(solution)/shard_map/all_to_all | solution.py:37
  258.8 91.0 %reduce-scatter.4.cloned.1.call-start = ((), (), s32[]{:S(2)}) async-start(), calls=%async_computation.12 | async-start | bytes 2359296 | tf_op jit(solution)/shard_map/reduce_scatter | solution.py:151
  298.9 3.6 copy-start.15
  308.3 2.3 copy-start.16
  311.4 6.6 %copy-start.22 = (f32[2,512,128]{2,1,0:T(8,128)S(1)}, f32[2,512,128]{2,1,0:T(8,128)}, u32[]{:S(2)}) copy-start(f32[2,512,128]{2,1,0:T(8,128)} %copy-done.21) | copy-start | bytes 1572868
  312.3 42.0 %all-to-all-start.4 = ((f32[16,72,128]{2,1,0:T(8,128)}), f32[16,72,128]{2,1,0:T(8,128)S(1)}, u32[]{:S(2)}, u32[]{:S(2)}) async-start(f32[16,72,128]{2,1,0:T(8,128)} %bitcast.202), calls=%async_computation.4 | async-start | bytes 1179648 | tf_op jit(solution)/shard_map/all_to_all | solution.py:37
  319.2 31.8 %collective-permute-start.1 = (f32[256,512]{1,0:T(8,128)S(1)}, f32[256,512]{1,0:T(8,128)S(1)}, u32[]{:S(2)}, u32[]{:S(2)}) collective-permute-start(f32[256,512]{1,0:T(8,128)S(1)} %bitcast.207), channel_id=1, source_target_pairs={{0,1},{1,0},{2,3},{3,2},{4,5},{5,4},{6,7},{7,6},{8,9},{9,8},{10,11... | collective-permute-start | bytes 1572872 | tf_op jit(solution)/shard_map/ppermute | solution.py:46
  324.8 28.5 %collective-permute-start.4 = (f32[8,64,128]{2,1,0:T(8,128)}, f32[8,64,128]{2,1,0:T(8,128)}, u32[]{:S(2)}, u32[]{:S(2)}) collective-permute-start(f32[8,64,128]{2,1,0:T(8,128)} %reduce-scatter.8.cloned.1.call-done), channel_id=1, source_target_pairs={{0,1},{1,0},{2,3},{3,2},{4,5},{5,4},{6,7},{7,6},{8,9},{9,8},{10,11... | collective-permute-start | bytes 786440 | tf_op jit(solution)/shard_map/ppermute | solution.py:153
  324.9 36.5 %collective-permute-start.3 = (f32[8,64,128]{2,1,0:T(8,128)}, f32[8,64,128]{2,1,0:T(8,128)S(1)}, u32[]{:S(2)}, u32[]{:S(2)}) collective-permute-start(f32[8,64,128]{2,1,0:T(8,128)} %reduce-scatter.6.cloned.1.call-done), channel_id=1, source_target_pairs={{0,1},{1,0},{2,3},{3,2},{4,5},{5,4},{6,7},{7,6},{8,9},{9,8},{10,11... | collective-permute-start | bytes 786440 | tf_op jit(solution)/shard_map/ppermute | solution.py:153
  349.8 11.7 %collective-permute-start.2 = (f32[8,64,128]{2,1,0:T(8,128)}, f32[8,64,128]{2,1,0:T(8,128)}, u32[]{:S(2)}, u32[]{:S(2)}) collective-permute-start(f32[8,64,128]{2,1,0:T(8,128)} %reduce-scatter.4.cloned.1.call-done), channel_id=1, source_target_pairs={{0,1},{1,0},{2,3},{3,2},{4,5},{5,4},{6,7},{7,6},{8,9},{9,8},{10,11... | collective-permute-start | bytes 786440 | tf_op jit(solution)/shard_map/ppermute | solution.py:153
  351.1 2.1 copy-start.30
  353.2 8.2 %copy-start.29 = (f32[8,64,128]{2,1,0:T(8,128)S(1)}, f32[8,64,128]{2,1,0:T(8,128)}, u32[]{:S(2)}) copy-start(f32[8,64,128]{2,1,0:T(8,128)} %reduce-scatter.6.cloned.1.call-done) | copy-start | bytes 786436
  353.3 8.2 %copy-start.31 = (f32[8,64,128]{2,1,0:T(8,128)S(1)}, f32[8,64,128]{2,1,0:T(8,128)}, u32[]{:S(2)}) copy-start(f32[8,64,128]{2,1,0:T(8,128)} %reduce-scatter.4.cloned.1.call-done) | copy-start | bytes 786436
  355.1 15.9 %all-to-all-start.5 = ((f32[8,72,128]{2,1,0:T(8,128)}), f32[8,72,128]{2,1,0:T(8,128)S(1)}, u32[]{:S(2)}, u32[]{:S(2)}) async-start(f32[8,72,128]{2,1,0:T(8,128)} %broadcast_in_dim.41), calls=%async_computation.5 | async-start | bytes 589824 | tf_op jit(solution)/shard_map/all_to_all | solution.py:37
Sparse Core Ops, SparseCore 0:
  14.1 29.4 all-gather.7
  79.0 48.1 all-gather.5
  129.4 27.2 all-gather.3
  201.6 42.8 reduce-scatter.7
  246.7 56.5 reduce-scatter.5
  305.4 44.3 reduce-scatter.3
